TPU v7x, 128 devices: a whole 4x4x4 slice. The times are simulated.
128 devices in a mesh: seq: 16 (over x, z), fsdp: 8 (over y, core).
Axes of the slice: x: 4, y: 4, z: 4, core: 2. Of those that a mesh axis runs over, the one named last changes fastest.
Arguments:
- queries: bfloat16 [8, 6144, 2048], P('fsdp', 'seq'), may hold values from -16 to 16
- key_states: bfloat16 [8, 6144, 2048], P('fsdp', 'seq'), may hold values from -16 to 16
- value_states: bfloat16 [8, 6144, 2048], P('fsdp', 'seq'), may hold values from -6 to 6
- residual: bfloat16 [8, 6144, 3072], P('fsdp', 'seq'), may hold values from -6 to 6
- upstream: bfloat16 [8, 6144, 3072], P('fsdp', 'seq'), may hold values from -6 to 6
- mod_gate: float32 [8, 3072], P('fsdp'), may hold values from 0.5 to 1.5
- out_bias: float32 [3072], replicated, may hold values from -3 to 3
- w_out: bfloat16 [2048, 3072], P('fsdp'), may hold values from -0.125 to 0.125
- neighbours: int32 [48, 9], replicated, may hold values from 0 to 47, as said below
- counts: int32 [48], replicated, may hold values from 3 to 9, as said below
- text_tiles: int32 [4], replicated, may hold values from 0 to 47, as said below
Outputs:
- block_out: bfloat16 [8, 6144, 3072], P('fsdp', 'seq')
- grad_queries: bfloat16 [8, 6144, 2048], P('fsdp', 'seq')
- grad_keys: bfloat16 [8, 6144, 2048], P('fsdp', 'seq')
- grad_values: bfloat16 [8, 6144, 2048], P('fsdp', 'seq')
Inputs may be any that keep to these rules, and one draw needn't show every extreme that they name: `neighbours`: each query tile that holds image tokens lists first, in its counts slots, the distinct image tiles within one row and one column of its own place in the image, itself included; the image tiles are the tiles not in text_tiles, in increasing order, laid out row by row with 8 to a row. A text tile lists 9 distinct image tiles. Slots at or after counts hold arbitrary image tiles. `counts`: every text tile has 9. `text_tiles`: Distinct, in increasing order; the last tile of a sequence is always one of them.
All inputs are finite; a program needn't handle non-finite values.
Results may differ from a plain program's by a relative error of at most 0.023.
Values may be sent and summed in bfloat16 or wider, within the bound.
A program may use at most 128 MiB of HBM per device.

v0:
```python
import math

import jax
import jax.numpy as jnp
from jax import lax
from jax.sharding import PartitionSpec as P

HD = 128
HEADS = 16
TILE = 128


def key_layout(neighbours, counts, text_tiles):
    tile_count = neighbours.shape[0]
    slot_count = neighbours.shape[1]
    text_count = text_tiles.shape[0]
    listing = jnp.concatenate(
        [neighbours, jnp.broadcast_to(text_tiles[None, :], (tile_count, text_count))], axis=1
    )
    nearby = jnp.arange(slot_count, dtype=jnp.int32)[None, :] < counts[:, None]
    live_slots = jnp.concatenate(
        [nearby, jnp.ones((tile_count, text_count), dtype=jnp.bool_)], axis=1
    )
    return (listing, live_slots)


def attend_tiles(
    query_tiles, key_tiles, value_tiles, upstream_tiles, listing, live_slots, tile_group
):
    tile_count, tile_len, head_count, head_dim = query_tiles.shape
    factor = 1.0 / math.sqrt(head_dim)

    def one_group(sums_in, group_start):
        key_sum, value_sum = sums_in
        query_part = lax.dynamic_slice_in_dim(query_tiles, group_start, tile_group, 0)
        upstream_part = lax.dynamic_slice_in_dim(upstream_tiles, group_start, tile_group, 0)
        picked = lax.dynamic_slice_in_dim(listing, group_start, tile_group, 0)
        alive_slots = lax.dynamic_slice_in_dim(live_slots, group_start, tile_group, 0)
        key_near = key_tiles[picked]
        value_near = value_tiles[picked]
        scores = (
            jnp.einsum(
                "qthe,qkshe->qhtks", query_part, key_near, preferred_element_type=jnp.float32
            )
            * factor
        )
        scores = jnp.where(alive_slots[:, None, None, :, None], scores, -jnp.inf)
        row_max = jnp.max(scores, axis=(3, 4), keepdims=True)
        exponent = jnp.exp(scores - row_max)
        attn_prob = exponent / jnp.sum(exponent, axis=(3, 4), keepdims=True)
        prob_half = attn_prob.astype(jnp.bfloat16)
        attended = jnp.einsum(
            "qhtks,qkshe->qthe", prob_half, value_near, preferred_element_type=jnp.float32
        ).astype(jnp.bfloat16)
        row_delta = jnp.sum(
            upstream_part.astype(jnp.float32) * attended.astype(jnp.float32), axis=3
        )
        row_delta = jnp.transpose(row_delta, (0, 2, 1))[:, :, :, None, None]
        prob_grad = jnp.einsum(
            "qthe,qkshe->qhtks", upstream_part, value_near, preferred_element_type=jnp.float32
        )
        score_grad = (attn_prob * (prob_grad - row_delta) * factor).astype(jnp.bfloat16)
        grad_query = jnp.einsum(
            "qhtks,qkshe->qthe", score_grad, key_near, preferred_element_type=jnp.float32
        ).astype(jnp.bfloat16)
        key_terms = jnp.einsum(
            "qhtks,qthe->qkshe", score_grad, query_part, preferred_element_type=jnp.float32
        )
        value_terms = jnp.einsum(
            "qhtks,qthe->qkshe", prob_half, upstream_part, preferred_element_type=jnp.float32
        )
        flat_ids = picked.reshape(-1)
        key_sum = key_sum.at[flat_ids].add(key_terms.reshape(-1, tile_len, head_count, head_dim))
        value_sum = value_sum.at[flat_ids].add(
            value_terms.reshape(-1, tile_len, head_count, head_dim)
        )
        return ((key_sum, value_sum), (attended, grad_query))

    zeros_sum = jnp.zeros((tile_count, tile_len, head_count, head_dim), jnp.float32)
    group_starts = jnp.arange(0, tile_count, tile_group, dtype=jnp.int32)
    (key_sum, value_sum), (attended, grad_query) = lax.scan(
        one_group, (zeros_sum, zeros_sum), group_starts
    )
    row_total = tile_count * tile_len
    return (
        attended.reshape(row_total, head_count, head_dim),
        grad_query.reshape(row_total, head_count, head_dim),
        key_sum.astype(jnp.bfloat16).reshape(row_total, head_count, head_dim),
        value_sum.astype(jnp.bfloat16).reshape(row_total, head_count, head_dim),
    )


def local(
    queries,
    key_states,
    value_states,
    residual,
    upstream,
    mod_gate,
    out_bias,
    w_out,
    neighbours,
    counts,
    text_tiles,
):
    tok_rows = queries.shape[1]
    feature_total = queries.shape[2]

    def split_heads(array_in):
        return array_in.reshape(tok_rows, HEADS, HD)

    head_query, head_key, head_value = (
        lax.all_to_all(split_heads(queries[0]), "seq", split_axis=1, concat_axis=0, tiled=True),
        lax.all_to_all(split_heads(key_states[0]), "seq", split_axis=1, concat_axis=0, tiled=True),
        lax.all_to_all(
            split_heads(value_states[0]), "seq", split_axis=1, concat_axis=0, tiled=True
        ),
    )
    scaled = (upstream[0].astype(jnp.float32) * mod_gate[0][None, :]).astype(jnp.bfloat16)
    d_attn = jnp.einsum(
        "td,rd->tr",
        scaled,
        lax.all_gather(w_out, "fsdp", axis=0, tiled=True),
        preferred_element_type=jnp.float32,
    ).astype(jnp.bfloat16)
    head_upstream = lax.all_to_all(
        split_heads(d_attn), "seq", split_axis=1, concat_axis=0, tiled=True
    )
    seq_len = head_query.shape[0]
    local_heads = head_query.shape[1]
    tile_count = seq_len // TILE
    tile_group = math.gcd(tile_count, max(1, 512 // TILE))
    listing, live_slots = key_layout(neighbours, counts, text_tiles)

    def as_tiles(array_in):
        return array_in.reshape(tile_count, TILE, local_heads, HD)

    attended, grad_query, grad_key, grad_value = attend_tiles(
        as_tiles(head_query),
        as_tiles(head_key),
        as_tiles(head_value),
        as_tiles(head_upstream),
        listing,
        live_slots,
        tile_group,
    )
    tok_attn, tok_query, tok_key, tok_value = (
        lax.all_to_all(attended, "seq", split_axis=0, concat_axis=1, tiled=True),
        lax.all_to_all(grad_query, "seq", split_axis=0, concat_axis=1, tiled=True),
        lax.all_to_all(grad_key, "seq", split_axis=0, concat_axis=1, tiled=True),
        lax.all_to_all(grad_value, "seq", split_axis=0, concat_axis=1, tiled=True),
    )
    attn_rows = tok_attn.reshape(tok_rows, feature_total)
    projected = jnp.dot(
        attn_rows,
        lax.all_gather(w_out, "fsdp", axis=0, tiled=True),
        preferred_element_type=jnp.float32,
    )
    block_out = (
        residual[0].astype(jnp.float32) + mod_gate[0][None, :] * (projected + out_bias[None, :])
    ).astype(jnp.bfloat16)
    return (
        block_out[None],
        tok_query.reshape(1, tok_rows, feature_total),
        tok_key.reshape(1, tok_rows, feature_total),
        tok_value.reshape(1, tok_rows, feature_total),
    )


def solution(mesh):
    return jax.shard_map(
        local,
        mesh=mesh,
        in_specs=(
            P("fsdp", "seq", None),
            P("fsdp", "seq", None),
            P("fsdp", "seq", None),
            P("fsdp", "seq", None),
            P("fsdp", "seq", None),
            P("fsdp", None),
            P(),
            P("fsdp", None),
            P(),
            P(),
            P(),
        ),
        out_specs=(
            P("fsdp", "seq", None),
            P("fsdp", "seq", None),
            P("fsdp", "seq", None),
            P("fsdp", "seq", None),
        ),
        check_vma=False,
    )
```

profile of v0, /device:TPU:30, one launch (start us, length us, event | category | flops | bytes accessed | tf_op | source)
XLA Modules:
  0.0 981.8 jit_solution(5848188944340019950)
XLA Ops:
  20.5 19.9 %all-to-all-done = bf16[384,16,128]{2,0,1:T(8,128)(2,1)S(1)} async-done(((bf16[384,16,128]{2,0,1:T(8,128)(2,1)}), bf16[384,16,128]{2,0,1:T(8,128)(2,1)S(1)}, u32[]{:S(2)}, u32[]{:S(2)}) %all-to-all-start) | async-done | bytes 1572896 | tf_op jit(solution)/shard_map/all_to_all | solution.py:113
  49.3 18.1 %all-to-all-done.1 = bf16[384,16,128]{0,2,1:T(8,128)(2,1)S(1)} async-done(((bf16[384,16,128]{0,2,1:T(8,128)(2,1)}), bf16[384,16,128]{0,2,1:T(8,128)(2,1)S(1)}, u32[]{:S(2)}, u32[]{:S(2)}) %all-to-all-start.1) | async-done | bytes 1572896 | tf_op jit(solution)/shard_map/all_to_all | solution.py:114
  103.1 14.4 %all-to-all-done.2 = bf16[384,16,128]{2,0,1:T(8,128)(2,1)} async-done(((bf16[384,16,128]{2,0,1:T(8,128)(2,1)}), bf16[384,16,128]{2,0,1:T(8,128)(2,1)}, u32[]{:S(2)}, u32[]{:S(2)}) %all-to-all-start.2) | async-done | bytes 1572896 | tf_op jit(solution)/shard_map/all_to_all | solution.py:126
  121.6 702.8 %while.16 = (s32[]{:T(128)}, f32[48,128,1,128]{3,1,0,2:T(8,128)}, f32[48,128,1,128]{3,1,0,2:T(8,128)}, bf16[12,4,128,1,128]{4,2,1,0,3:T(8,128)(2,1)}, bf16[12,4,...) while((s32[]{:T(128)}, f32[48,128,1,128]{3,1,0,2:T(8,128)}, ...), condition=%wide.region_6.7_spmd, body=%wide.region_0.6_spmd.sunk | while | flops 1332018944 | bytes 87586320 | solution.py:81
  145.4 11.9 %scatter_fusion.1 = f32[48,128,128]{2,1,0:T(8,128)} fusion(f32[48,128,128]{2,1,0:T(8,128)} %bitcast.191, s32[52]{0:T(128)S(1)} %fusion.66, f32[52,128,128]{2,1,0:T(8,128)S(1)} %copy.183), kind=kCustom, calls=%fused_computation.3.clone.1 | custom fusion | flops 851968 | bytes 10223824 | tf_op jit(solution)/shard_map/while/body/eval_jaxpr/scatter-add | solution.py:74
  166.6 12.0 %scatter_fusion = f32[48,128,128]{2,1,0:T(8,128)} fusion(f32[48,128,128]{2,1,0:T(8,128)} %bitcast.183, s32[52]{0:T(128)S(1)} %fusion.66, f32[52,128,128]{2,1,0:T(8,128)S(1)} %copy.182), kind=kCustom, calls=%fused_computation.2.clone.1 | custom fusion | flops 851968 | bytes 10223824 | tf_op jit(solution)/shard_map/while/body/eval_jaxpr/scatter-add | solution.py:73
  225.2 11.9 %scatter_fusion = f32[48,128,128]{2,1,0:T(8,128)} fusion(f32[48,128,128]{2,1,0:T(8,128)} %bitcast.183, s32[52]{0:T(128)S(1)} %fusion.66, f32[52,128,128]{2,1,0:T(8,128)S(1)} %copy.182), kind=kCustom, calls=%fused_computation.2.clone.1 | custom fusion | flops 851968 | bytes 10223824 | tf_op jit(solution)/shard_map/while/body/eval_jaxpr/scatter-add | solution.py:73
  262.5 11.9 %scatter_fusion.1 = f32[48,128,128]{2,1,0:T(8,128)} fusion(f32[48,128,128]{2,1,0:T(8,128)} %bitcast.191, s32[52]{0:T(128)S(1)} %fusion.66, f32[52,128,128]{2,1,0:T(8,128)S(1)} %copy.183), kind=kCustom, calls=%fused_computation.3.clone.1 | custom fusion | flops 851968 | bytes 10223824 | tf_op jit(solution)/shard_map/while/body/eval_jaxpr/scatter-add | solution.py:74
  283.7 11.9 %scatter_fusion = f32[48,128,128]{2,1,0:T(8,128)} fusion(f32[48,128,128]{2,1,0:T(8,128)} %bitcast.183, s32[52]{0:T(128)S(1)} %fusion.66, f32[52,128,128]{2,1,0:T(8,128)S(1)} %copy.182), kind=kCustom, calls=%fused_computation.2.clone.1 | custom fusion | flops 851968 | bytes 10223824 | tf_op jit(solution)/shard_map/while/body/eval_jaxpr/scatter-add | solution.py:73
  321.0 12.0 %scatter_fusion.1 = f32[48,128,128]{2,1,0:T(8,128)} fusion(f32[48,128,128]{2,1,0:T(8,128)} %bitcast.191, s32[52]{0:T(128)S(1)} %fusion.66, f32[52,128,128]{2,1,0:T(8,128)S(1)} %copy.183), kind=kCustom, calls=%fused_computation.3.clone.1 | custom fusion | flops 851968 | bytes 10223824 | tf_op jit(solution)/shard_map/while/body/eval_jaxpr/scatter-add | solution.py:74
  342.3 12.0 %scatter_fusion = f32[48,128,128]{2,1,0:T(8,128)} fusion(f32[48,128,128]{2,1,0:T(8,128)} %bitcast.183, s32[52]{0:T(128)S(1)} %fusion.66, f32[52,128,128]{2,1,0:T(8,128)S(1)} %copy.182), kind=kCustom, calls=%fused_computation.2.clone.1 | custom fusion | flops 851968 | bytes 10223824 | tf_op jit(solution)/shard_map/while/body/eval_jaxpr/scatter-add | solution.py:73
  379.7 11.9 %scatter_fusion.1 = f32[48,128,128]{2,1,0:T(8,128)} fusion(f32[48,128,128]{2,1,0:T(8,128)} %bitcast.191, s32[52]{0:T(128)S(1)} %fusion.66, f32[52,128,128]{2,1,0:T(8,128)S(1)} %copy.183), kind=kCustom, calls=%fused_computation.3.clone.1 | custom fusion | flops 851968 | bytes 10223824 | tf_op jit(solution)/shard_map/while/body/eval_jaxpr/scatter-add | solution.py:74
  400.9 12.0 %scatter_fusion = f32[48,128,128]{2,1,0:T(8,128)} fusion(f32[48,128,128]{2,1,0:T(8,128)} %bitcast.183, s32[52]{0:T(128)S(1)} %fusion.66, f32[52,128,128]{2,1,0:T(8,128)S(1)} %copy.182), kind=kCustom, calls=%fused_computation.2.clone.1 | custom fusion | flops 851968 | bytes 10223824 | tf_op jit(solution)/shard_map/while/body/eval_jaxpr/scatter-add | solution.py:73
  438.4 11.9 %scatter_fusion.1 = f32[48,128,128]{2,1,0:T(8,128)} fusion(f32[48,128,128]{2,1,0:T(8,128)} %bitcast.191, s32[52]{0:T(128)S(1)} %fusion.66, f32[52,128,128]{2,1,0:T(8,128)S(1)} %copy.183), kind=kCustom, calls=%fused_computation.3.clone.1 | custom fusion | flops 851968 | bytes 10223824 | tf_op jit(solution)/shard_map/while/body/eval_jaxpr/scatter-add | solution.py:74
  459.6 11.9 %scatter_fusion = f32[48,128,128]{2,1,0:T(8,128)} fusion(f32[48,128,128]{2,1,0:T(8,128)} %bitcast.183, s32[52]{0:T(128)S(1)} %fusion.66, f32[52,128,128]{2,1,0:T(8,128)S(1)} %copy.182), kind=kCustom, calls=%fused_computation.2.clone.1 | custom fusion | flops 851968 | bytes 10223824 | tf_op jit(solution)/shard_map/while/body/eval_jaxpr/scatter-add | solution.py:73
  496.9 11.9 %scatter_fusion.1 = f32[48,128,128]{2,1,0:T(8,128)} fusion(f32[48,128,128]{2,1,0:T(8,128)} %bitcast.191, s32[52]{0:T(128)S(1)} %fusion.66, f32[52,128,128]{2,1,0:T(8,128)S(1)} %copy.183), kind=kCustom, calls=%fused_computation.3.clone.1 | custom fusion | flops 851968 | bytes 10223824 | tf_op jit(solution)/shard_map/while/body/eval_jaxpr/scatter-add | solution.py:74
  518.2 12.0 %scatter_fusion = f32[48,128,128]{2,1,0:T(8,128)} fusion(f32[48,128,128]{2,1,0:T(8,128)} %bitcast.183, s32[52]{0:T(128)S(1)} %fusion.66, f32[52,128,128]{2,1,0:T(8,128)S(1)} %copy.182), kind=kCustom, calls=%fused_computation.2.clone.1 | custom fusion | flops 851968 | bytes 10223824 | tf_op jit(solution)/shard_map/while/body/eval_jaxpr/scatter-add | solution.py:73
  555.5 11.9 %scatter_fusion.1 = f32[48,128,128]{2,1,0:T(8,128)} fusion(f32[48,128,128]{2,1,0:T(8,128)} %bitcast.191, s32[52]{0:T(128)S(1)} %fusion.66, f32[52,128,128]{2,1,0:T(8,128)S(1)} %copy.183), kind=kCustom, calls=%fused_computation.3.clone.1 | custom fusion | flops 851968 | bytes 10223824 | tf_op jit(solution)/shard_map/while/body/eval_jaxpr/scatter-add | solution.py:74
  576.8 12.0 %scatter_fusion = f32[48,128,128]{2,1,0:T(8,128)} fusion(f32[48,128,128]{2,1,0:T(8,128)} %bitcast.183, s32[52]{0:T(128)S(1)} %fusion.66, f32[52,128,128]{2,1,0:T(8,128)S(1)} %copy.182), kind=kCustom, calls=%fused_computation.2.clone.1 | custom fusion | flops 851968 | bytes 10223824 | tf_op jit(solution)/shard_map/while/body/eval_jaxpr/scatter-add | solution.py:73
  635.3 11.9 %scatter_fusion = f32[48,128,128]{2,1,0:T(8,128)} fusion(f32[48,128,128]{2,1,0:T(8,128)} %bitcast.183, s32[52]{0:T(128)S(1)} %fusion.66, f32[52,128,128]{2,1,0:T(8,128)S(1)} %copy.182), kind=kCustom, calls=%fused_computation.2.clone.1 | custom fusion | flops 851968 | bytes 10223824 | tf_op jit(solution)/shard_map/while/body/eval_jaxpr/scatter-add | solution.py:73
  693.7 12.0 %scatter_fusion = f32[48,128,128]{2,1,0:T(8,128)} fusion(f32[48,128,128]{2,1,0:T(8,128)} %bitcast.183, s32[52]{0:T(128)S(1)} %fusion.66, f32[52,128,128]{2,1,0:T(8,128)S(1)} %copy.182), kind=kCustom, calls=%fused_computation.2.clone.1 | custom fusion | flops 851968 | bytes 10223824 | tf_op jit(solution)/shard_map/while/body/eval_jaxpr/scatter-add | solution.py:73
  752.2 11.9 %scatter_fusion = f32[48,128,128]{2,1,0:T(8,128)} fusion(f32[48,128,128]{2,1,0:T(8,128)} %bitcast.183, s32[52]{0:T(128)S(1)} %fusion.66, f32[52,128,128]{2,1,0:T(8,128)S(1)} %copy.182), kind=kCustom, calls=%fused_computation.2.clone.1 | custom fusion | flops 851968 | bytes 10223824 | tf_op jit(solution)/shard_map/while/body/eval_jaxpr/scatter-add | solution.py:73
  789.5 11.9 %scatter_fusion.1 = f32[48,128,128]{2,1,0:T(8,128)} fusion(f32[48,128,128]{2,1,0:T(8,128)} %bitcast.191, s32[52]{0:T(128)S(1)} %fusion.66, f32[52,128,128]{2,1,0:T(8,128)S(1)} %copy.183), kind=kCustom, calls=%fused_computation.3.clone.1 | custom fusion | flops 851968 | bytes 10223824 | tf_op jit(solution)/shard_map/while/body/eval_jaxpr/scatter-add | solution.py:74
  810.7 12.0 %scatter_fusion = f32[48,128,128]{2,1,0:T(8,128)} fusion(f32[48,128,128]{2,1,0:T(8,128)} %bitcast.183, s32[52]{0:T(128)S(1)} %fusion.66, f32[52,128,128]{2,1,0:T(8,128)S(1)} %copy.182), kind=kCustom, calls=%fused_computation.2.clone.1 | custom fusion | flops 851968 | bytes 10223824 | tf_op jit(solution)/shard_map/while/body/eval_jaxpr/scatter-add | solution.py:73
  (465 shorter events, 651.7 us)
Async XLA Ops:
  7.2 70.4 %all-gather.2.cloned.1.call-start = ((), (), s32[]{:S(2)}) async-start(), calls=%async_computation.8 | async-start | bytes 14155776 | tf_op jit(solution)/shard_map/all_gather | solution.py:123
  10.5 29.9 %all-to-all-start = ((bf16[384,16,128]{2,0,1:T(8,128)(2,1)}), bf16[384,16,128]{2,0,1:T(8,128)(2,1)S(1)}, u32[]{:S(2)}, u32[]{:S(2)}) async-start(bf16[384,16,128]{2,0,1:T(8,128)(2,1)} %copy.122), calls=%async_computation | async-start | bytes 3145728 | tf_op jit(solution)/shard_map/all_to_all | solution.py:113
  20.5 27.2 %copy-start.10 = (bf16[1,384,2048]{2,1,0:T(8,128)(2,1)S(1)}, bf16[1,384,2048]{2,1,0:T(8,128)(2,1)}, u32[]{:S(2)}) copy-start(bf16[1,384,2048]{2,1,0:T(8,128)(2,1)} %param.15) | copy-start | bytes 4718596
  41.6 25.8 %all-to-all-start.1 = ((bf16[384,16,128]{0,2,1:T(8,128)(2,1)}), bf16[384,16,128]{0,2,1:T(8,128)(2,1)S(1)}, u32[]{:S(2)}, u32[]{:S(2)}) async-start(bf16[384,16,128]{0,2,1:T(8,128)(2,1)} %bitcast.41), calls=%async_computation.1 | async-start | bytes 3145728 | tf_op jit(solution)/shard_map/all_to_all | solution.py:114
  49.3 28.2 %copy-start.14 = (f32[1,3072]{1,0:T(1,128)S(1)}, f32[1,3072]{1,0:T(1,128)}, u32[]{:S(2)}) copy-start(f32[1,3072]{1,0:T(1,128)} %param.18) | copy-start | bytes 36868
  67.4 24.5 %all-to-all-start.3 = ((bf16[384,16,128]{0,2,1:T(8,128)(2,1)}), bf16[384,16,128]{0,2,1:T(8,128)(2,1)S(1)}, u32[]{:S(2)}, u32[]{:S(2)}) async-start(bf16[384,16,128]{0,2,1:T(8,128)(2,1)} %bitcast.204), calls=%async_computation.3 | async-start | bytes 3145728 | tf_op jit(solution)/shard_map/all_to_all | solution.py:115
  87.9 10.3 %copy-start.17 = (s32[4]{0:T(128)S(1)}, s32[4]{0:T(128)}, u32[]{:S(2)}) copy-start(s32[4]{0:T(128)} %param.23) | copy-start | bytes 52
  87.9 10.4 %copy-start.12 = (s32[48,9]{0,1:T(8,128)S(1)}, s32[48,9]{0,1:T(8,128)}, u32[]{:S(2)}) copy-start(s32[48,9]{0,1:T(8,128)} %param.21) | copy-start | bytes 5188
  87.9 11.2 %copy-start.13 = (s32[48]{0:T(128)S(1)}, s32[48]{0:T(128)}, u32[]{:S(2)}) copy-start(s32[48]{0:T(128)} %param.22) | copy-start | bytes 580
  91.9 25.6 %all-to-all-start.2 = ((bf16[384,16,128]{2,0,1:T(8,128)(2,1)}), bf16[384,16,128]{2,0,1:T(8,128)(2,1)}, u32[]{:S(2)}, u32[]{:S(2)}) async-start(bf16[384,16,128]{2,0,1:T(8,128)(2,1)} %bitcast.203), calls=%async_computation.2 | async-start | bytes 3145728 | tf_op jit(solution)/shard_map/all_to_all | solution.py:126
  185.2 9.9 %copy-start.1 = (bf16[4,128,1,128]{3,1,0,2:T(8,128)(2,1)}, bf16[4,128,1,128]{3,1,0,2:T(8,128)(2,1)S(1)}, u32[]{:S(2)}) copy-start(bf16[4,128,1,128]{3,1,0,2:T(8,128)(2,1)S(1)} %constant_dynamic-slice_fusion.6) | copy-start | bytes 393220 | tf_op jit(solution)/shard_map/while
  243.7 9.8 %copy-start.1 = (bf16[4,128,1,128]{3,1,0,2:T(8,128)(2,1)}, bf16[4,128,1,128]{3,1,0,2:T(8,128)(2,1)S(1)}, u32[]{:S(2)}) copy-start(bf16[4,128,1,128]{3,1,0,2:T(8,128)(2,1)S(1)} %constant_dynamic-slice_fusion.6) | copy-start | bytes 393220 | tf_op jit(solution)/shard_map/while
  360.9 9.9 %copy-start.1 = (bf16[4,128,1,128]{3,1,0,2:T(8,128)(2,1)}, bf16[4,128,1,128]{3,1,0,2:T(8,128)(2,1)S(1)}, u32[]{:S(2)}) copy-start(bf16[4,128,1,128]{3,1,0,2:T(8,128)(2,1)S(1)} %constant_dynamic-slice_fusion.6) | copy-start | bytes 393220 | tf_op jit(solution)/shard_map/while
  419.6 9.9 %copy-start.1 = (bf16[4,128,1,128]{3,1,0,2:T(8,128)(2,1)}, bf16[4,128,1,128]{3,1,0,2:T(8,128)(2,1)S(1)}, u32[]{:S(2)}) copy-start(bf16[4,128,1,128]{3,1,0,2:T(8,128)(2,1)S(1)} %constant_dynamic-slice_fusion.6) | copy-start | bytes 393220 | tf_op jit(solution)/shard_map/while
  478.2 9.9 %copy-start.1 = (bf16[4,128,1,128]{3,1,0,2:T(8,128)(2,1)}, bf16[4,128,1,128]{3,1,0,2:T(8,128)(2,1)S(1)}, u32[]{:S(2)}) copy-start(bf16[4,128,1,128]{3,1,0,2:T(8,128)(2,1)S(1)} %constant_dynamic-slice_fusion.6) | copy-start | bytes 393220 | tf_op jit(solution)/shard_map/while
  536.8 9.9 %copy-start.1 = (bf16[4,128,1,128]{3,1,0,2:T(8,128)(2,1)}, bf16[4,128,1,128]{3,1,0,2:T(8,128)(2,1)S(1)}, u32[]{:S(2)}) copy-start(bf16[4,128,1,128]{3,1,0,2:T(8,128)(2,1)S(1)} %constant_dynamic-slice_fusion.6) | copy-start | bytes 393220 | tf_op jit(solution)/shard_map/while
  595.3 9.9 %copy-start.1 = (bf16[4,128,1,128]{3,1,0,2:T(8,128)(2,1)}, bf16[4,128,1,128]{3,1,0,2:T(8,128)(2,1)S(1)}, u32[]{:S(2)}) copy-start(bf16[4,128,1,128]{3,1,0,2:T(8,128)(2,1)S(1)} %constant_dynamic-slice_fusion.6) | copy-start | bytes 393220 | tf_op jit(solution)/shard_map/while
  653.8 9.9 %copy-start.1 = (bf16[4,128,1,128]{3,1,0,2:T(8,128)(2,1)}, bf16[4,128,1,128]{3,1,0,2:T(8,128)(2,1)S(1)}, u32[]{:S(2)}) copy-start(bf16[4,128,1,128]{3,1,0,2:T(8,128)(2,1)S(1)} %constant_dynamic-slice_fusion.6) | copy-start | bytes 393220 | tf_op jit(solution)/shard_map/while
  712.3 9.8 %copy-start.1 = (bf16[4,128,1,128]{3,1,0,2:T(8,128)(2,1)}, bf16[4,128,1,128]{3,1,0,2:T(8,128)(2,1)S(1)}, u32[]{:S(2)}) copy-start(bf16[4,128,1,128]{3,1,0,2:T(8,128)(2,1)S(1)} %constant_dynamic-slice_fusion.6) | copy-start | bytes 393220 | tf_op jit(solution)/shard_map/while
  770.7 9.9 %copy-start.1 = (bf16[4,128,1,128]{3,1,0,2:T(8,128)(2,1)}, bf16[4,128,1,128]{3,1,0,2:T(8,128)(2,1)S(1)}, u32[]{:S(2)}) copy-start(bf16[4,128,1,128]{3,1,0,2:T(8,128)(2,1)S(1)} %constant_dynamic-slice_fusion.6) | copy-start | bytes 393220 | tf_op jit(solution)/shard_map/while
  829.7 24.4 %all-to-all-start.5 = ((bf16[16,2,24576]{2,1,0:T(2,128)(2,1)}), bf16[16,2,24576]{2,1,0:T(2,128)(2,1)S(1)}, u32[]{:S(2)}, u32[]{:S(2)}) async-start(bf16[16,2,24576]{2,1,0:T(2,128)(2,1)} %reshape.233), calls=%async_computation.5 | async-start | bytes 3145728 | tf_op jit(solution)/shard_map/all_to_all | solution.py:149
  854.1 25.7 %all-to-all-start.6 = ((bf16[16,2,24576]{2,1,0:T(2,128)(2,1)}), bf16[16,2,24576]{2,1,0:T(2,128)(2,1)S(1)}, u32[]{:S(2)}, u32[]{:S(2)}) async-start(bf16[16,2,24576]{2,1,0:T(2,128)(2,1)} %reshape.235), calls=%async_computation.6 | async-start | bytes 3145728 | tf_op jit(solution)/shard_map/all_to_all | solution.py:150
  879.8 25.1 %all-to-all-start.4 = ((bf16[16,2,24576]{2,1,0:T(2,128)(2,1)}), bf16[16,2,24576]{2,1,0:T(2,128)(2,1)S(1)}, u32[]{:S(2)}, u32[]{:S(2)}) async-start(bf16[16,2,24576]{2,1,0:T(2,128)(2,1)} %reshape.231), calls=%async_computation.4 | async-start | bytes 3145728 | tf_op jit(solution)/shard_map/all_to_all | solution.py:148
  906.0 44.3 %all-to-all-start.7 = ((bf16[16,2,24576]{2,1,0:T(2,128)(2,1)}), bf16[16,2,24576]{2,1,0:T(2,128)(2,1)}, u32[]{:S(2)}, u32[]{:S(2)}) async-start(bf16[16,2,24576]{2,1,0:T(2,128)(2,1)} %reshape.237), calls=%async_computation.7 | async-start | bytes 3145728 | tf_op jit(solution)/shard_map/all_to_all | solution.py:151
  (47 other events, 95.2 us)
Sparse Core Ops, SparseCore 0:
  9.7 67.7 all-gather.1
where the time goes:
time: 997 us; the launch traced here: 982 us
  other arithmetic  326 us (33%)
  local copies, waits for them, and re-layouts  303 us (30%)
  matrix products  168 us (17%)
  waiting for transfers between devices  94.4 us (9%)
  starting transfers between devices  51 us (5%)
  loops' own time  24.5 us (2%)
  between operations  14.2 us (1%)
    scatter-add x12, other arithmetic, one_group(): key_sum.at[flat_ids]  144 us
    scatter-add x12, other arithmetic, one_group(): value_sum.at[flat_ids]  143 us
    unnamed x46, local copies, waits for them, and re-layouts  57.6 us
    dot_general x12, matrix products, one_group(): jnp.einsum('qhtks,qthe->qkshe', score_grad, query_part, preferred_element...  47.4 us
    reshape x12, local copies, waits for them, and re-layouts, one_group(): value_terms.reshape(-1, tile_len, head_count, head_dim)  42.9 us
    reshape x12, local copies, waits for them, and re-layouts, one_group(): key_terms.reshape(-1, tile_len, head_count, head_dim)  42.9 us
    dynamic_update_slice x36, local copies, waits for them, and re-layouts, attend_tiles(): lax.scan(one_group, (zeros_sum, zeros_sum), group_starts)  41 us
    dot_general x12, matrix products, one_group(): jnp.einsum('qhtks,qthe->qkshe', prob_half, upstream_part, preferred_eleme...  33.9 us
  transfers between devices with their start and end apart: 9, of which 8 were waited for; matrix products, arithmetic and copies ran while one was open for 8% of the time, Pallas kernels for 0%

commit v1 on v0

v1 whole, which is shorter than its diff:
```python
import math
import jax, jax.numpy as jnp
from jax import lax
from jax.experimental import pallas as pl
from jax.experimental.pallas import tpu as pltpu
from jax.sharding import PartitionSpec as P

HD=128; TILE=128; TILES=48; NBR=9; TXT=4; SLOTS=13
FACTOR = 1.0/math.sqrt(HD)
EXP2 = FACTOR*math.log2(math.e)
F32=jnp.float32; BF=jnp.bfloat16

def tables(neighbours, counts, text_tiles):
    ids = jnp.arange(TILES, dtype=jnp.int32)
    slot = jnp.arange(NBR, dtype=jnp.int32)
    live = slot[None, :] < counts[:, None]
    near = jnp.where(live, neighbours, neighbours[:, :1])
    keys = jnp.concatenate([near, jnp.broadcast_to(text_tiles[None, :], (TILES, TXT))], axis=1)
    bias = jnp.where(live, 0.0, -jnp.inf).astype(F32)
    hit = (neighbours[:, :, None] == ids[None, None, :]) & live[:, :, None]
    block = jnp.sum(jnp.where(hit, (slot[None, :, None] + 1) + SLOTS * ids[:, None, None], 0), axis=1)
    is_text = jnp.any(ids[:, None] == text_tiles[None, :], axis=1)
    who = jnp.concatenate([near, jnp.broadcast_to(text_tiles[None, :], (TILES, TXT))], axis=1)
    ok = jnp.concatenate([live, jnp.ones((TILES, TXT), jnp.bool_)], axis=1) & ~is_text[:, None]
    pick = jnp.sum(jnp.where(who[:, :, None] == ids[None, None, :], block.T[:, None, :], 0), axis=2)
    pidx = jnp.where(ok & (pick > 0), pick - 1, TILES * SLOTS)
    tsel = jnp.min(jnp.where(ids[:, None] == text_tiles[None, :], jnp.arange(TXT, dtype=jnp.int32)[None, :], TXT), axis=1)
    return keys, bias, pidx, tsel

def tile(ref, i):
    return ref[pl.ds(pl.multiple_of(i * TILE, TILE), TILE), :]

NT = (((1,), (1,)), ((), ()))
NN = (((1,), (0,)), ((), ()))

def dot(a, b, dims=NN):
    return lax.dot_general(a, b, dims, preferred_element_type=F32)

def fwd_tile(i, q_ref, k_ref, vt_ref, keys_ref, bias_ref, p_ref, s_ref, inv_ref, attn_ref):
    q = tile(q_ref, i)
    top = None
    kc = jnp.concatenate([tile(k_ref, keys_ref[i, s]) for s in range(SLOTS)], axis=0)
    sall = dot(kc, q, NT).reshape(SLOTS, TILE, TILE)
    for s in range(SLOTS):
        sc = sall[s]
        s_ref[s] = sc
        top = sc if top is None else jnp.maximum(top, sc)
    m = jnp.max(top, axis=0, keepdims=True) * EXP2
    total = None
    parts = []
    for s in range(SLOTS):
        shift = m if s < 3 or s >= NBR else m - bias_ref[i, s]
        e = jnp.exp2(s_ref[s] * EXP2 - shift)
        total = e if total is None else total + e
        e16 = e.astype(BF)
        p_ref[i * SLOTS + s] = e16
        parts.append(e16)
    inv = 1.0 / jnp.sum(total, axis=0, keepdims=True)
    inv_ref[i] = inv
    pt = jnp.concatenate(parts, axis=0)
    vt = jnp.concatenate([vt_ref[keys_ref[i, s]] for s in range(SLOTS)], axis=1)
    attn_t = dot(vt, pt) * inv
    attn_ref[pl.ds(pl.multiple_of(i * TILE, TILE), TILE), :] = attn_t.astype(BF).T

def key_tile(j, who_ref, pidx_ref, tsel_ref, p_ref, x_ref, text_ref, out_ref):
    lhs = jnp.concatenate([p_ref[pidx_ref[j, r]] for r in range(SLOTS)], axis=1)
    rhs = jnp.concatenate([tile(x_ref, who_ref[j, r]) for r in range(SLOTS)], axis=0)
    acc = dot(lhs, rhs) + text_ref[tsel_ref[j]]
    out_ref[pl.ds(pl.multiple_of(j * TILE, TILE), TILE), :] = acc.astype(BF)

def text_keys(p_ref, x_ref, text_ref):
    G = 12
    text_ref[...] = jnp.zeros_like(text_ref)
    def body(g, _):
        rhs = x_ref[pl.ds(pl.multiple_of(g * G * TILE, TILE), G * TILE), :]
        for u in range(TXT):
            lhs = jnp.concatenate([p_ref[(g * G + n) * SLOTS + NBR + u] for n in range(G)], axis=1)
            text_ref[u] += dot(lhs, rhs)
        return 0
    lax.fori_loop(0, TILES // G, body, 0)

def bwd_tile(i, v_ref, kt_ref, do_ref, attn_ref, keys_ref, p_ref, inv_ref, dq_ref):
    do = tile(do_ref, i)
    prod = do.astype(F32) * tile(attn_ref, i).astype(F32)
    delta = jnp.sum(prod.T, axis=0, keepdims=True)
    c = inv_ref[i] * FACTOR
    dc = delta * c
    vc = jnp.concatenate([tile(v_ref, keys_ref[i, s]) for s in range(SLOTS)], axis=0)
    dpall = dot(vc, do, NT).reshape(SLOTS, TILE, TILE)
    parts = [(p_ref[i * SLOTS + s].astype(F32) * (dpall[s] * c - dc)).astype(BF) for s in range(SLOTS)]
    for s in range(SLOTS): p_ref[i * SLOTS + s] = parts[s]
    ds = jnp.concatenate(parts, axis=0)
    kt = jnp.concatenate([kt_ref[keys_ref[i, s]] for s in range(SLOTS)], axis=1)
    dq_t = dot(kt, ds)
    dq_ref[pl.ds(pl.multiple_of(i * TILE, TILE), TILE), :] = dq_t.astype(BF).T

def scale_rows(i, do_ref, inv_ref, dos_ref):
    col = jnp.broadcast_to(inv_ref[i], (TILE, TILE)).T
    sl = pl.ds(pl.multiple_of(i * TILE, TILE), TILE)
    dos_ref[sl, :] = (do_ref[sl, :].astype(F32) * col).astype(BF)

def attn_kernel(keys_ref, bias_ref, pidx_ref, tsel_ref, q_ref, k_ref, v_ref, do_ref, attn_ref, dq_ref, dk_ref, dv_ref,
                p_ref, s_ref, kt_ref, vt_ref, inv_ref, text_ref, dos_ref):
    p_ref[TILES * SLOTS] = jnp.zeros((TILE, TILE), BF)
    def loop(n, f, unroll=1):
        lax.fori_loop(0, n, lambda i, _: (f(i), 0)[1], 0, unroll=unroll)
    def tr(j):
        kt_ref[j] = tile(k_ref, j).T
        vt_ref[j] = tile(v_ref, j).T
    if True:
        loop(TILES, tr, 4)
    if True:
        loop(TILES, lambda i: fwd_tile(i, q_ref, k_ref, vt_ref, keys_ref, bias_ref, p_ref, s_ref, inv_ref, attn_ref), 4)
    if True:
        loop(TILES, lambda i: scale_rows(i, do_ref, inv_ref, dos_ref), 4)
        text_keys(p_ref, dos_ref, text_ref)
    if True:
        loop(TILES, lambda j: key_tile(j, keys_ref, pidx_ref, tsel_ref, p_ref, dos_ref, text_ref, dv_ref), 4)
    if True:
        loop(TILES, lambda i: bwd_tile(i, v_ref, kt_ref, do_ref, attn_ref, keys_ref, p_ref, inv_ref, dq_ref), 4)
    if True:
        text_keys(p_ref, q_ref, text_ref)
    if True:
        loop(TILES, lambda j: key_tile(j, keys_ref, pidx_ref, tsel_ref, p_ref, q_ref, text_ref, dk_ref), 4)

def attention(tabs, q, k, v, do):
    n = TILES * TILE
    V = pl.BlockSpec(memory_space=pltpu.VMEM); S = pl.BlockSpec(memory_space=pltpu.SMEM)
    return pl.pallas_call(attn_kernel,
        out_shape=[jax.ShapeDtypeStruct((n, HD), BF)] * 4,
        in_specs=[S]*4 + [V]*4, out_specs=[V]*4,
        scratch_shapes=[pltpu.VMEM((TILES*SLOTS+1, TILE, TILE), BF), pltpu.VMEM((SLOTS, TILE, TILE), F32),
            pltpu.VMEM((TILES, TILE, TILE), BF), pltpu.VMEM((TILES, TILE, TILE), BF), pltpu.VMEM((TILES, 1, TILE), F32),
            pltpu.VMEM((TXT+1, TILE, TILE), F32), pltpu.VMEM((n, HD), BF)],
        compiler_params=pltpu.CompilerParams(vmem_limit_bytes=60<<20), name="attention_core",
        )(*tabs, q, k, v, do)


def local(queries, key_states, value_states, residual, upstream, mod_gate, out_bias, w_out, neighbours, counts, text_tiles):
    def to_heads(x):
        return lax.all_to_all(x, "seq", split_axis=1, concat_axis=0, tiled=True)

    def to_tokens(x):
        return lax.all_to_all(x, "seq", split_axis=0, concat_axis=1, tiled=True)

    w = lax.all_gather(w_out, "fsdp", axis=0, tiled=True)
    tabs = tables(neighbours, counts, text_tiles)
    q, k, v = to_heads(queries[0]), to_heads(key_states[0]), to_heads(value_states[0])
    scaled = (upstream[0].astype(F32) * mod_gate[0][None, :]).astype(BF)
    d_attn = dot(scaled, w, NT).astype(BF)
    do = to_heads(d_attn)
    attn, dq, dk, dv = attention(tabs, q, k, v, do)
    attn, dq, dk, dv = [to_tokens(x) for x in (attn, dq, dk, dv)]
    projected = dot(attn, w)
    block_out = (residual[0].astype(F32) + mod_gate[0][None, :] * (projected + out_bias[None, :])).astype(BF)
    return block_out[None], dq[None], dk[None], dv[None]


def solution(mesh):
    act = P("fsdp", "seq", None)
    return jax.shard_map(local, mesh=mesh, in_specs=(act,) * 5 + (P("fsdp", None), P(), P("fsdp", None), P(), P(), P()),
                         out_specs=(act,) * 4, check_vma=False)
```

time: 997 us -> 298 us (0.30); the launches traced: 982 us -> 297 us
  other arithmetic: 326 us -> 3.18 us
  local copies, waits for them, and re-layouts: 303 us -> 33.3 us
  matrix products: 168 us -> 18.9 us
  Pallas kernels: 0 us -> 67.1 us
  blocking collectives: 0 us -> 47.3 us
  loops' own time: 24.5 us -> 0 us
  waiting for transfers between devices: 94.4 us -> 74.3 us
  starting transfers between devices: 51 us -> 38.8 us
    scatter-add x24 -> x0, other arithmetic: 286 us -> none  [the longest x12 144 us: one_group(): key_sum.at[flat_ids]]
    dot_general x74 -> x2, matrix products: 168 us -> 18.9 us  [dot(): return lax.dot_general(a, b, dims, preferred_element_type=F32)]
    reshape x38 -> x0, local copies, waits for them, and re-layouts: 89 us -> none  [the longest x12 42.9 us: one_group(): value_terms.reshape(-1, tile_len, head_count, head_dim)]
    pallas_call x0 -> x1, Pallas kernels: none -> 67.1 us  [attention(): pl.pallas_call(attn_kernel, out_shape=[jax.ShapeDtypeStruct((n, HD), BF)]...]
    gather x24 -> x0, local copies, waits for them, and re-layouts: 54.7 us -> none  [the longest x12 27.4 us: one_group(): value_near = value_tiles[picked]]
    unnamed x46 -> x30, local copies, waits for them, and re-layouts: 57.6 us -> 8.01 us
    all_to_all x0 -> x2, blocking collectives: none -> 47.3 us  [to_tokens(): return lax.all_to_all(x, 'seq', split_axis=0, concat_axis=1, tiled=True)]
    dynamic_update_slice x36 -> x0, local copies, waits for them, and re-layouts: 41 us -> none  [attend_tiles(): lax.scan(one_group, (zeros_sum, zeros_sum), group_starts)]
  transfers between devices with their start and end apart: 9 -> 7, of which waited for: 8 -> 6; matrix products, arithmetic and copies ran while one was open for 8% -> 13% of each run, Pallas kernels for 0% -> 0%
where the time goes in v1:
time: 298 us; the launch traced here: 297 us
  waiting for transfers between devices  74.3 us (25%)
  Pallas kernels  67.1 us (23%)
  blocking collectives  47.3 us (16%)
  starting transfers between devices  38.8 us (13%)
  local copies, waits for them, and re-layouts  33.3 us (11%)
  matrix products  18.9 us (6%)
  between operations  14.1 us (5%)
  other arithmetic  3.18 us (1%)
    pallas_call x1, Pallas kernels, attention(): pl.pallas_call(attn_kernel, out_shape=[jax.ShapeDtypeStruct((n, HD), BF)]...  67.1 us
    all_to_all x4, waiting for transfers between devices, to_heads(): return lax.all_to_all(x, 'seq', split_axis=1, concat_axis=0, tiled=True)  57.1 us
    all_to_all x2, blocking collectives, to_tokens(): return lax.all_to_all(x, 'seq', split_axis=0, concat_axis=1, tiled=True)  47.3 us
    all_to_all x4, starting transfers between devices, to_heads(): return lax.all_to_all(x, 'seq', split_axis=1, concat_axis=0, tiled=True)  26.4 us
    dot_general x2, matrix products, dot(): return lax.dot_general(a, b, dims, preferred_element_type=F32)  18.9 us
    all_to_all x2, waiting for transfers between devices, to_tokens(): return lax.all_to_all(x, 'seq', split_axis=0, concat_axis=1, tiled=True)  13.6 us
    all_to_all x2, starting transfers between devices, to_tokens(): return lax.all_to_all(x, 'seq', split_axis=0, concat_axis=1, tiled=True)  12.4 us
    broadcast_in_dim x3, local copies, waits for them, and re-layouts, local(): return (block_out[None], dq[None], dk[None], dv[None])  9.42 us
  transfers between devices with their start and end apart: 7, of which 6 were waited for; matrix products, arithmetic and copies ran while one was open for 13% of the time, Pallas kernels for 0%

profile of v1, /device:TPU:30, one launch (start us, length us, event | category | flops | bytes accessed | tf_op | source)
XLA Modules:
  0.0 297.0 jit_solution(14711344743460790336)
XLA Ops:
  10.5 8.4 %all-to-all-start = ((bf16[384,16,128]{2,0,1:T(8,128)(2,1)}), bf16[384,16,128]{2,0,1:T(8,128)(2,1)S(1)}, u32[]{:S(2)}, u32[]{:S(2)}) async-start(bf16[384,16,128]{2,0,1:T(8,128)(2,1)} %copy.53), calls=%async_computation | async-start | bytes 3145728 | tf_op jit(solution)/shard_map/all_to_all | solution.py:141
  20.9 19.5 %all-to-all-done = bf16[384,16,128]{2,0,1:T(8,128)(2,1)S(1)} async-done(((bf16[384,16,128]{2,0,1:T(8,128)(2,1)}), bf16[384,16,128]{2,0,1:T(8,128)(2,1)S(1)}, u32[]{:S(2)}, u32[]{:S(2)}) %all-to-all-start) | async-done | bytes 1572896 | tf_op jit(solution)/shard_map/all_to_all | solution.py:141
  41.6 6.1 %all-to-all-start.1 = ((bf16[384,16,128]{2,0,1:T(8,128)(2,1)}), bf16[384,16,128]{2,0,1:T(8,128)(2,1)S(1)}, u32[]{:S(2)}, u32[]{:S(2)}) async-start(bf16[384,16,128]{2,0,1:T(8,128)(2,1)} %copy.54), calls=%async_computation.1 | async-start | bytes 3145728 | tf_op jit(solution)/shard_map/all_to_all | solution.py:141
  47.8 1.8 copy.64
  51.2 16.2 %all-to-all-done.1 = bf16[384,16,128]{2,0,1:T(8,128)(2,1)S(1)} async-done(((bf16[384,16,128]{2,0,1:T(8,128)(2,1)}), bf16[384,16,128]{2,0,1:T(8,128)(2,1)S(1)}, u32[]{:S(2)}, u32[]{:S(2)}) %all-to-all-start.1) | async-done | bytes 1572896 | tf_op jit(solution)/shard_map/all_to_all | solution.py:141
  68.6 6.0 %all-to-all-start.2 = ((bf16[384,16,128]{2,0,1:T(8,128)(2,1)}), bf16[384,16,128]{2,0,1:T(8,128)(2,1)S(1)}, u32[]{:S(2)}, u32[]{:S(2)}) async-start(bf16[384,16,128]{2,0,1:T(8,128)(2,1)} %copy.55), calls=%async_computation.2 | async-start | bytes 3145728 | tf_op jit(solution)/shard_map/all_to_all | solution.py:141
  74.7 2.9 all-gather.2.cloned.1.call-done
  77.5 8.8 %fusion.6 = bf16[48,16,8,128]{3,2,1,0:T(8,128)(2,1)S(1)} fusion(bf16[2048,3072]{1,0:T(8,128)(2,1)} %all-gather.2.cloned.1.call-done, bf16[1,384,3072]{2,1,0:T(8,128)(2,1)} %param.15, f32[3072]{0:T(1024)S(1)} %bitcast.74), kind=kOutput, calls=%fused_computation.9 | convolution fusion | flops 4836163584 | bytes 16527360 | tf_op jit(solution)/shard_map/dot_general | solution.py:37
  87.9 5.1 %all-to-all-done.2 = bf16[384,16,128]{2,0,1:T(8,128)(2,1)S(1)} async-done(((bf16[384,16,128]{2,0,1:T(8,128)(2,1)}), bf16[384,16,128]{2,0,1:T(8,128)(2,1)S(1)}, u32[]{:S(2)}, u32[]{:S(2)}) %all-to-all-start.2) | async-done | bytes 1572896 | tf_op jit(solution)/shard_map/all_to_all | solution.py:141
  94.2 5.8 %all-to-all-start.3 = ((bf16[384,16,128]{2,0,1:T(8,128)(2,1)}), bf16[384,16,128]{2,0,1:T(8,128)(2,1)S(1)}, u32[]{:S(2)}, u32[]{:S(2)}) async-start(bf16[384,16,128]{2,0,1:T(8,128)(2,1)} %bitcast.55), calls=%async_computation.3 | async-start | bytes 3145728 | tf_op jit(solution)/shard_map/all_to_all | solution.py:141
  103.5 16.3 %all-to-all-done.3 = bf16[384,16,128]{2,0,1:T(8,128)(2,1)S(1)} async-done(((bf16[384,16,128]{2,0,1:T(8,128)(2,1)}), bf16[384,16,128]{2,0,1:T(8,128)(2,1)S(1)}, u32[]{:S(2)}, u32[]{:S(2)}) %all-to-all-start.3) | async-done | bytes 1572896 | tf_op jit(solution)/shard_map/all_to_all | solution.py:141
  120.9 67.1 %attention_core.1 = (bf16[6144,128]{1,0:T(8,128)(2,1)}, bf16[6144,128]{1,0:T(8,128)(2,1)}, bf16[6144,128]{1,0:T(8,128)(2,1)}, bf16[6144,128]{1,0:T(8,128)(2,1)}) custom-call(s32[48,13]{1,0:T(8,128)} %copy-done.7, f32[48,9]{1,0:T(8,128)} %fusion.11.bias_ref, s32[48,13]{1,0:T(8,128)} %add_select_fusion.pidx_ref, s32[48]{0:T(128)} %select_reduce_fusion.2.tsel_ref, ...), custom_call_target="tpu_custom_call" | custom-call | tf_op jit(solution)/shard_map/attention_core/pallas_call | solution.py:129
  188.0 25.0 %all_to_all.143 = bf16[16,384,128]{2,1,0:T(8,128)(2,1)} all-to-all(bf16[16,384,128]{2,1,0:T(8,128)(2,1)} %bitcast.72), channel_id=1, replica_groups=mesh['seq'=16,'fsdp'=8] {'seq'}, dimensions={0} | all-to-all | bytes 3145728 | tf_op jit(solution)/shard_map/all_to_all | solution.py:144
  213.0 22.3 %all_to_all.144 = bf16[16,384,128]{2,1,0:T(8,128)(2,1)S(1)} all-to-all(bf16[16,384,128]{2,1,0:T(8,128)(2,1)S(1)} %bitcast.71), channel_id=1, replica_groups=mesh['seq'=16,'fsdp'=8] {'seq'}, dimensions={0} | all-to-all | bytes 3145728 | tf_op jit(solution)/shard_map/all_to_all | solution.py:144
  235.3 5.7 %all-to-all-start.7 = ((bf16[16,384,128]{2,1,0:T(8,128)(2,1)}), bf16[16,384,128]{2,1,0:T(8,128)(2,1)S(1)}, u32[]{:S(2)}, u32[]{:S(2)}) async-start(bf16[16,384,128]{2,1,0:T(8,128)(2,1)} %bitcast.70), calls=%async_computation.7 | async-start | bytes 3145728 | tf_op jit(solution)/shard_map/all_to_all | solution.py:144
  241.0 2.6 copy.57
  243.6 13.6 %all-to-all-done.7 = bf16[16,384,128]{2,1,0:T(8,128)(2,1)S(1)} async-done(((bf16[16,384,128]{2,1,0:T(8,128)(2,1)}), bf16[16,384,128]{2,1,0:T(8,128)(2,1)S(1)}, u32[]{:S(2)}, u32[]{:S(2)}) %all-to-all-start.7) | async-done | bytes 1572896 | tf_op jit(solution)/shard_map/all_to_all | solution.py:144
  257.2 6.7 %all-to-all-start.4 = ((bf16[16,384,128]{1,2,0:T(8,128)(2,1)}), bf16[16,384,128]{1,2,0:T(8,128)(2,1)}, u32[]{:S(2)}, u32[]{:S(2)}) async-start(bf16[16,384,128]{1,2,0:T(8,128)(2,1)} %copy.57), calls=%async_computation.4 | async-start | bytes 3145728 | tf_op jit(solution)/shard_map/all_to_all | solution.py:144
  263.8 3.6 %copy.58 = bf16[384,16,128]{2,1,0:T(8,128)(2,1)} copy(bf16[384,16,128]{2,0,1:T(8,128)(2,1)} %bitcast.58) | data formatting | bytes 3145728 | tf_op jit(solution)/shard_map/all_to_all | solution.py:144
  267.4 3.7 %broadcast_in_dim.111 = bf16[1,384,2048]{2,1,0:T(8,128)(2,1)} reshape(bf16[384,16,128]{2,1,0:T(8,128)(2,1)} %copy.58) | data formatting | bytes 3145728 | tf_op jit(solution)/shard_map/broadcast_in_dim | solution.py:156
  271.1 2.2 copy.59
  273.2 3.7 %broadcast_in_dim.112 = bf16[1,384,2048]{2,1,0:T(8,128)(2,1)} reshape(bf16[384,16,128]{2,1,0:T(8,128)(2,1)} %copy.59) | data formatting | bytes 3145728 | tf_op jit(solution)/shard_map/broadcast_in_dim | solution.py:156
  278.0 2.1 broadcast_in_dim.113
  280.0 10.1 %fusion.2 = bf16[1,384,3072]{2,1,0:T(8,128)(2,1)} fusion(bf16[384,2048]{0,1:T(8,128)(2,1)} %bitcast.15, bf16[2048,3072]{1,0:T(8,128)(2,1)} %all-gather.2.cloned.1.call-done, bf16[1,384,3072]{2,1,0:T(8,128)(2,1)} %param.14, f32[3072]{0:T(1024)S(1)} %copy-done.12, f32[3072]{0:T(1024)S(1)} %bitcast.75), kind=kOutput, calls=%fused_computation.4 | convolution fusion | flops 4837736448 | bytes 18898944 | tf_op jit(solution)/shard_map/dot_general | solution.py:37
  (56 shorter events, 17.6 us)
Async XLA Ops:
  7.2 1.4 copy-start.4
  7.2 70.4 %all-gather.2.cloned.1.call-start = ((), (), s32[]{:S(2)}) async-start(), calls=%async_computation.8 | async-start | bytes 14155776 | tf_op jit(solution)/shard_map/all_gather | solution.py:146
  10.5 8.4 %copy-start.5 = (bf16[1,384,2048]{2,1,0:T(8,128)(2,1)S(1)}, bf16[1,384,2048]{2,1,0:T(8,128)(2,1)}, u32[]{:S(2)}) copy-start(bf16[1,384,2048]{2,1,0:T(8,128)(2,1)} %param.12) | copy-start | bytes 4718596
  10.5 29.9 %all-to-all-start = ((bf16[384,16,128]{2,0,1:T(8,128)(2,1)}), bf16[384,16,128]{2,0,1:T(8,128)(2,1)S(1)}, u32[]{:S(2)}, u32[]{:S(2)}) async-start(bf16[384,16,128]{2,0,1:T(8,128)(2,1)} %copy.53), calls=%async_computation | async-start | bytes 3145728 | tf_op jit(solution)/shard_map/all_to_all | solution.py:141
  40.5 1.1 copy-start
  41.6 25.8 %all-to-all-start.1 = ((bf16[384,16,128]{2,0,1:T(8,128)(2,1)}), bf16[384,16,128]{2,0,1:T(8,128)(2,1)S(1)}, u32[]{:S(2)}, u32[]{:S(2)}) async-start(bf16[384,16,128]{2,0,1:T(8,128)(2,1)} %copy.54), calls=%async_computation.1 | async-start | bytes 3145728 | tf_op jit(solution)/shard_map/all_to_all | solution.py:141
  51.2 23.3 %copy-start.9 = (s32[48]{0:T(128)S(1)}, s32[48]{0:T(128)}, u32[]{:S(2)}) copy-start(s32[48]{0:T(128)} %param.20) | copy-start | bytes 580
  51.2 26.3 %copy-start.11 = (f32[1,3072]{1,0:T(1,128)S(1)}, f32[1,3072]{1,0:T(1,128)}, u32[]{:S(2)}) copy-start(f32[1,3072]{1,0:T(1,128)} %param.16) | copy-start | bytes 36868
  67.4 1.1 copy-start.1
  68.6 24.5 %all-to-all-start.2 = ((bf16[384,16,128]{2,0,1:T(8,128)(2,1)}), bf16[384,16,128]{2,0,1:T(8,128)(2,1)S(1)}, u32[]{:S(2)}, u32[]{:S(2)}) async-start(bf16[384,16,128]{2,0,1:T(8,128)(2,1)} %copy.55), calls=%async_computation.2 | async-start | bytes 3145728 | tf_op jit(solution)/shard_map/all_to_all | solution.py:141
  93.0 1.1 copy-start.2
  93.0 6.9 %copy-start.10 = (s32[4]{0:T(128)S(1)}, s32[4]{0:T(128)}, u32[]{:S(2)}) copy-start(s32[4]{0:T(128)} %param.21) | copy-start | bytes 52
  93.0 7.2 %copy-start.8 = (s32[48,9]{0,1:T(8,128)S(1)}, s32[48,9]{0,1:T(8,128)}, u32[]{:S(2)}) copy-start(s32[48,9]{0,1:T(8,128)} %param.19) | copy-start | bytes 5188
  94.2 25.6 %all-to-all-start.3 = ((bf16[384,16,128]{2,0,1:T(8,128)(2,1)}), bf16[384,16,128]{2,0,1:T(8,128)(2,1)S(1)}, u32[]{:S(2)}, u32[]{:S(2)}) async-start(bf16[384,16,128]{2,0,1:T(8,128)(2,1)} %bitcast.55), calls=%async_computation.3 | async-start | bytes 3145728 | tf_op jit(solution)/shard_map/all_to_all | solution.py:141
  100.8 19.0 %copy-start.7 = (s32[48,13]{1,0:T(8,128)}, s32[48,13]{1,0:T(8,128)S(1)}, u32[]{:S(2)}) copy-start(s32[48,13]{1,0:T(8,128)S(1)} %pad_add_fusion.keys_ref) | copy-start | bytes 7492
  119.8 1.1 copy-start.3
  188.0 25.0 %copy-start.6 = (bf16[6144,128]{1,0:T(8,128)(2,1)S(1)}, bf16[6144,128]{1,0:T(8,128)(2,1)}, u32[]{:S(2)}) copy-start(bf16[6144,128]{1,0:T(8,128)(2,1)} %get-tuple-element.10) | copy-start | bytes 4718596
  235.3 21.9 %all-to-all-start.7 = ((bf16[16,384,128]{2,1,0:T(8,128)(2,1)}), bf16[16,384,128]{2,1,0:T(8,128)(2,1)S(1)}, u32[]{:S(2)}, u32[]{:S(2)}) async-start(bf16[16,384,128]{2,1,0:T(8,128)(2,1)} %bitcast.70), calls=%async_computation.7 | async-start | bytes 3145728 | tf_op jit(solution)/shard_map/all_to_all | solution.py:144
  257.2 22.9 %all-to-all-start.4 = ((bf16[16,384,128]{1,2,0:T(8,128)(2,1)}), bf16[16,384,128]{1,2,0:T(8,128)(2,1)}, u32[]{:S(2)}, u32[]{:S(2)}) async-start(bf16[16,384,128]{1,2,0:T(8,128)(2,1)} %copy.57), calls=%async_computation.4 | async-start | bytes 3145728 | tf_op jit(solution)/shard_map/all_to_all | solution.py:144
  278.0 2.1 copy-start.12
Sparse Core Ops, SparseCore 0:
  9.7 67.7 all-gather.1

commit v2 on v1

v2 whole, which is shorter than its diff:
```python
import math
import jax, jax.numpy as jnp
from jax import lax
from jax.experimental import pallas as pl
from jax.experimental.pallas import tpu as pltpu
from jax.sharding import PartitionSpec as P

HD=128; TILE=128; TILES=48; NBR=9; TXT=4; SLOTS=13; D=3072; SEQ=6144; HDT=2048
FACTOR = 1.0/math.sqrt(HD)
EXP2 = FACTOR*math.log2(math.e)
F32=jnp.float32; BF=jnp.bfloat16

def table_kernel(text_ref, near_ref, near_t_ref, count_ref, count_t_ref, keys_ref, bias_ref, pidx_ref, tsel_ref):
    near, near_t, count, count_t = near_ref[...], near_t_ref[...], count_ref[...], count_t_ref[...]
    live = lax.broadcasted_iota(jnp.int32, (TILES, NBR), 1) < count
    keys_ref[:, :NBR] = jnp.where(live, near, near[:, :1])
    bias_ref[...] = jnp.where(live, 0.0, -jnp.inf).astype(F32)
    query = lax.broadcasted_iota(jnp.int32, (TILES, TILES), 0)
    key = lax.broadcasted_iota(jnp.int32, (TILES, TILES), 1)
    block = jnp.zeros((TILES, TILES), jnp.int32)
    for s in range(NBR):
        block = jnp.where((near[:, s:s + 1] == key) & (s < count), query * SLOTS + s + 1, block)
    ids = lax.broadcasted_iota(jnp.int32, (1, TILES), 1)
    tsel = jnp.full((1, TILES), TXT, jnp.int32)
    for u in range(TXT):
        keys_ref[:, NBR + u:NBR + u + 1] = jnp.full((TILES, 1), text_ref[u], jnp.int32)
        tsel = jnp.where(ids == text_ref[u], u, tsel)
    tsel_ref[...] = tsel
    for r in range(SLOTS):
        who = near_t[r:r + 1, :] if r < NBR else jnp.full((1, TILES), text_ref[r - NBR], jnp.int32)
        pick = jnp.sum(jnp.where(query == who, block, 0), axis=0, keepdims=True)
        ok = (pick > 0) & (tsel == TXT)
        if r < NBR:
            ok = ok & (r < count_t)
        pidx_ref[r:r + 1, :] = jnp.where(ok, pick - 1, TILES * SLOTS)


def tables(neighbours, counts, text_tiles):
    S, V = [pl.BlockSpec(memory_space=m) for m in (pltpu.SMEM, pltpu.VMEM)]
    i32 = jnp.int32
    return pl.pallas_call(
        table_kernel,
        out_shape=[jax.ShapeDtypeStruct((TILES, SLOTS), i32), jax.ShapeDtypeStruct((TILES, NBR), F32),
                   jax.ShapeDtypeStruct((SLOTS, TILES), i32), jax.ShapeDtypeStruct((1, TILES), i32)],
        in_specs=[S] + [V] * 4, out_specs=[V] * 4, name="tables",
    )(text_tiles, neighbours, neighbours.T, counts[:, None], counts[None, :])


def tile(ref, i):
    return ref[i]

NT = (((1,), (1,)), ((), ()))
NN = (((1,), (0,)), ((), ()))

def dot(a, b, dims=NN):
    return lax.dot_general(a, b, dims, preferred_element_type=F32)

def fwd_tile(i, q_ref, k_ref, vt_ref, keys_ref, bias_ref, p_ref, s_ref, inv_ref, attn_ref):
    q = tile(q_ref, i)
    top = None
    kc = jnp.concatenate([tile(k_ref, keys_ref[i, s]) for s in range(SLOTS)], axis=0)
    sall = dot(kc, q, NT).reshape(SLOTS, TILE, TILE)
    for s in range(SLOTS):
        sc = sall[s]
        s_ref[s] = sc
        top = sc if top is None else jnp.maximum(top, sc)
    m = jnp.max(top, axis=0, keepdims=True) * EXP2
    total = None
    parts = []
    for s in range(SLOTS):
        shift = m if s < 3 or s >= NBR else m - bias_ref[i, s]
        e = jnp.exp2(s_ref[s] * EXP2 - shift)
        total = e if total is None else total + e
        e16 = e.astype(BF)
        p_ref[i * SLOTS + s] = e16
        parts.append(e16)
    inv = 1.0 / jnp.sum(total, axis=0, keepdims=True)
    inv_ref[i] = inv
    pt = jnp.concatenate(parts, axis=0)
    vt = jnp.concatenate([vt_ref[keys_ref[i, s]] for s in range(SLOTS)], axis=1)
    attn_t = dot(vt, pt) * inv
    attn_ref[i] = attn_t.astype(BF).T

def key_tile(j, who_ref, pidx_ref, tsel_ref, p_ref, x_ref, text_ref, out_ref):
    lhs = jnp.concatenate([p_ref[pidx_ref[r, j]] for r in range(SLOTS)], axis=1)
    rhs = jnp.concatenate([tile(x_ref, who_ref[j, r]) for r in range(SLOTS)], axis=0)
    acc = dot(lhs, rhs) + text_ref[tsel_ref[0, j]]
    out_ref[j] = acc.astype(BF)

def text_keys(p_ref, x_ref, text_ref):
    G = 12
    text_ref[...] = jnp.zeros_like(text_ref)
    def body(g, _):
        rhs = x_ref[pl.ds(g * G, G)].reshape(G * TILE, HD)
        for u in range(TXT):
            lhs = jnp.concatenate([p_ref[(g * G + n) * SLOTS + NBR + u] for n in range(G)], axis=1)
            text_ref[u] += dot(lhs, rhs)
        return 0
    lax.fori_loop(0, TILES // G, body, 0)

def bwd_tile(i, v_ref, kt_ref, do_ref, attn_ref, keys_ref, p_ref, inv_ref, dq_ref):
    do = tile(do_ref, i)
    prod = do.astype(F32) * tile(attn_ref, i).astype(F32)
    delta = jnp.sum(prod.T, axis=0, keepdims=True)
    c = inv_ref[i] * FACTOR
    dc = delta * c
    vc = jnp.concatenate([tile(v_ref, keys_ref[i, s]) for s in range(SLOTS)], axis=0)
    dpall = dot(vc, do, NT).reshape(SLOTS, TILE, TILE)
    parts = [(p_ref[i * SLOTS + s].astype(F32) * (dpall[s] * c - dc)).astype(BF) for s in range(SLOTS)]
    for s in range(SLOTS): p_ref[i * SLOTS + s] = parts[s]
    ds = jnp.concatenate(parts, axis=0)
    kt = jnp.concatenate([kt_ref[keys_ref[i, s]] for s in range(SLOTS)], axis=1)
    dq_t = dot(kt, ds)
    dq_ref[i] = dq_t.astype(BF).T

def scale_rows(i, do_ref, inv_ref, dos_ref):
    col = jnp.broadcast_to(inv_ref[i], (TILE, TILE)).T
    dos_ref[i] = (do_ref[i].astype(F32) * col).astype(BF)


MESH = pl.DeviceIdType.MESH
PEERS = 16
ROWS = SEQ // PEERS
SHARD = 256
OWN = TILES // PEERS
K_, V_, Q_, O_, AT_, DV_, DQ_, DK_ = range(8)


def rows_of(p):
    return pl.ds(p * OWN, OWN)


def head_of(p):
    return pl.ds(pl.multiple_of(p * HD, HD), HD)


def block_kernel(keys_ref, bias_ref, pidx_ref, tsel_ref, gate_ref, obias_ref,
                 q_in, k_in, v_in, res_in, up_in, w_in,
                 out_ref, dq_out, dk_out, dv_out,
                 q_ref, k_ref, v_ref, do_ref, at_land, w_ref, up_ref, sc_ref, dst_ref,
                 at_st, dv_st, dq_st, dk_st,
                 p_ref, s_ref, kt_ref, vt_ref, inv_ref, text_ref,
                 send, recv, own, wsend, wrecv, lsem):
    me = lax.axis_index("seq")
    mx, mz = me // 4, me % 4
    f = lax.axis_index("fsdp")
    y, c = f // 2, f % 2
    sib = y * 2 + (1 - c)
    yup = ((y + 1) % 4) * 2 + c
    ydn = ((y + 3) % 4) * 2 + c
    far = ((y + 2) % 4) * 2 + c

    def peer(n):
        return ((mx + n // 4) % 4) * 4 + (mz + n % 4) % 4

    def loop(n, body, lo=0):
        lax.fori_loop(lo, n, lambda i, _: (body(i), 0)[1], 0)

    def wrows(shard, off=0, n=SHARD):
        return pl.ds(pl.multiple_of(shard * SHARD + off, 128), n)

    def to_head(a, src, land, p):
        return pltpu.make_async_remote_copy(src.at[:, :, head_of(p)], land.at[rows_of(me)], send.at[a, p], recv.at[a, me],
                                            device_id={"seq": p}, device_id_type=MESH)

    def to_rows(a, src, land, p):
        return pltpu.make_async_remote_copy(src.at[rows_of(p)], land.at[:, :, head_of(me)], send.at[a, p], recv.at[a, me],
                                            device_id={"seq": p}, device_id_type=MESH)

    def got_head(a, src, land, p):
        pltpu.make_async_remote_copy(src.at[:, :, head_of(p)], land.at[rows_of(p)], send.at[a, p], recv.at[a, p],
                                     device_id={"seq": p}, device_id_type=MESH).wait_recv()

    def got_rows(a, src, land, p):
        pltpu.make_async_remote_copy(src.at[rows_of(p)], land.at[:, :, head_of(p)], send.at[a, p], recv.at[a, p],
                                     device_id={"seq": p}, device_id_type=MESH).wait_recv()

    def own_head(a, src, land):
        return pltpu.make_async_copy(src.at[:, :, head_of(me)], land.at[rows_of(me)], own.at[a])

    def own_rows(a, src, land):
        return pltpu.make_async_copy(src.at[rows_of(me)], land.at[:, :, head_of(me)], own.at[a])

    def wcopy(k, shard, target, src=None, off=0, n=SHARD):
        part = w_ref.at[wrows(shard, off, n)]
        return pltpu.make_async_remote_copy(part if src is None else src, part, wsend.at[k], wrecv.at[k],
                                            device_id={"fsdp": target}, device_id_type=MESH)

    get_up = pltpu.make_async_copy(up_in, up_ref, lsem.at[0])
    get_up.start()
    get_w = pltpu.make_async_copy(w_in, w_ref.at[wrows(f)], lsem.at[1])
    get_w.start()

    barrier = pltpu.get_barrier_semaphore()
    loop(PEERS, lambda n: pl.semaphore_signal(barrier, inc=1, device_id={"seq": peer(n)}, device_id_type=MESH), 1)
    for t in (sib, yup, ydn):
        pl.semaphore_signal(barrier, inc=1, device_id={"fsdp": t}, device_id_type=MESH)
    pl.semaphore_wait(barrier, PEERS + 2)

    w_up = wcopy(0, f, yup, w_in)
    w_dn = wcopy(1, f, ydn, w_in)
    w_sib = wcopy(4, f, sib, w_in)
    w_up.start()
    w_dn.start()
    w_sib.start()
    for a, src, land in ((K_, k_in, k_ref), (V_, v_in, v_ref), (Q_, q_in, q_ref)):
        own_head(a, src, land).start()
        loop(PEERS, lambda n, a=a, src=src, land=land: to_head(a, src, land, peer(n)).start(), 1)

    p_ref[TILES * SLOTS] = jnp.zeros((TILE, TILE), BF)
    get_up.wait()

    def scale_up(g):
        sl = pl.ds(pl.multiple_of(g * 32, 32), 32)
        sc_ref[sl, :] = (up_ref[sl, :].astype(F32) * gate_ref[...]).astype(BF)

    loop(ROWS // 32, scale_up)
    get_res = pltpu.make_async_copy(res_in, up_ref, lsem.at[0])
    get_res.start()

    def d_attn(shard):
        r = dot(sc_ref[...], w_ref[wrows(shard), :], NT).astype(BF)
        dst_ref[:, :, pl.ds(pl.multiple_of(shard * SHARD, SHARD), SHARD)] = r.reshape(OWN, TILE, SHARD)

    get_w.wait()
    d_attn(f)
    w_sib.wait_recv()
    d_attn(sib)

    def turn(src, dst):
        def body(n):
            p = peer(n)
            for t in range(3):
                dst[p * 3 + t] = tile(src, p * 3 + t).T
        return body

    own_head(K_, k_in, k_ref).wait()
    loop(PEERS, lambda n: got_head(K_, k_in, k_ref, peer(n)), 1)
    loop(PEERS, turn(k_ref, kt_ref))
    w_up.wait_recv()
    fwd_up = wcopy(2, ydn, yup, None, 0, 128)
    fwd_up.start()
    sh_dn = wcopy(5, ydn, sib)
    sh_dn.start()
    w_dn.wait_recv()
    fwd_dn = wcopy(3, yup, ydn, None, 128, 128)
    fwd_dn.start()
    sh_up = wcopy(6, yup, sib)
    sh_up.start()
    d_attn(ydn)
    d_attn(yup)
    own_head(V_, v_in, v_ref).wait()
    loop(PEERS, lambda n: got_head(V_, v_in, v_ref, peer(n)), 1)
    loop(PEERS, turn(v_ref, vt_ref))
    sh_dn.wait_recv()
    d_attn(ydn + 1 - 2 * c)
    sh_up.wait_recv()
    d_attn(yup + 1 - 2 * c)
    wcopy(2, far, yup, None, 0, 128).wait_recv()
    wcopy(3, far, yup, None, 128, 128).wait_recv()
    sh_far = wcopy(7, far, sib)
    sh_far.start()
    d_attn(far)
    own_head(Q_, q_in, q_ref).wait()
    loop(PEERS, lambda n: got_head(Q_, q_in, q_ref, peer(n)), 1)
    sh_far.wait_recv()
    d_attn(far + 1 - 2 * c)
    own_head(O_, dst_ref, do_ref).start()
    loop(PEERS, lambda n: to_head(O_, dst_ref, do_ref, peer(n)).start(), 1)

    def stage(a, st, land, per_tile):
        def body(n):
            p = peer(n)
            for t in range(3):
                per_tile(p * 3 + t)

            @pl.when(n < PEERS)
            def _():
                to_rows(a, st, land, p).start()

        loop(PEERS + 1, body, 1)
        own_rows(a, st, land).start()

    stage(AT_, at_st, at_land, lambda i: fwd_tile(i, q_ref, k_ref, vt_ref, keys_ref, bias_ref, p_ref, s_ref, inv_ref, at_st))
    own_head(O_, dst_ref, do_ref).wait()
    loop(PEERS, lambda n: got_head(O_, dst_ref, do_ref, peer(n)), 1)
    lax.fori_loop(0, TILES, lambda i, _: (scale_rows(i, do_ref, inv_ref, dq_st), 0)[1], 0, unroll=4)
    text_keys(p_ref, dq_st, text_ref)
    stage(DV_, dv_st, dv_out, lambda j: key_tile(j, keys_ref, pidx_ref, tsel_ref, p_ref, dq_st, text_ref, dv_st))
    stage(DQ_, dq_st, dq_out, lambda i: bwd_tile(i, v_ref, kt_ref, do_ref, at_st, keys_ref, p_ref, inv_ref, dq_st))
    text_keys(p_ref, q_ref, text_ref)
    stage(DK_, dk_st, dk_out, lambda j: key_tile(j, keys_ref, pidx_ref, tsel_ref, p_ref, q_ref, text_ref, dk_st))

    own_rows(AT_, at_st, at_land).wait()
    loop(PEERS, lambda n: got_rows(AT_, at_st, at_land, peer(n)), 1)
    get_res.wait()

    def project(g):
        sl = pl.ds(pl.multiple_of(g * 256, 256), 256)
        acc = dot(at_land[...].reshape(ROWS, HDT), w_ref[:, sl]) + obias_ref[:, sl]
        sc_ref[:, sl] = (up_ref[:, sl].astype(F32) + gate_ref[:, sl] * acc).astype(BF)

    loop(D // 256, project)
    put = pltpu.make_async_copy(sc_ref, out_ref, lsem.at[1])
    put.start()

    outs = ((DV_, dv_st, dv_out), (DQ_, dq_st, dq_out), (DK_, dk_st, dk_out))
    for a, st, land in outs:
        own_rows(a, st, land).wait()
        loop(PEERS, lambda n, a=a, st=st, land=land: got_rows(a, st, land, peer(n)), 1)
    for cp in (w_up, w_dn, w_sib, fwd_up, fwd_dn, sh_dn, sh_up, sh_far):
        cp.wait_send()
    for a, src, land in ((K_, k_in, k_ref), (V_, v_in, v_ref), (Q_, q_in, q_ref), (O_, dst_ref, do_ref)):
        loop(PEERS, lambda n, a=a, src=src, land=land: to_head(a, src, land, peer(n)).wait_send(), 1)
    for a, st, land in ((AT_, at_st, at_land),) + outs:
        loop(PEERS, lambda n, a=a, st=st, land=land: to_rows(a, st, land, peer(n)).wait_send(), 1)
    put.wait()


def local(queries, key_states, value_states, residual, upstream, mod_gate, out_bias, w_out, neighbours, counts, text_tiles):
    tabs = tables(neighbours, counts, text_tiles)
    S, V, A = [pl.BlockSpec(memory_space=m) for m in (pltpu.SMEM, pltpu.VMEM, pl.ANY)]
    head = pltpu.VMEM((TILES, TILE, HD), BF)
    tok = pltpu.VMEM((ROWS, D), BF)
    mid = pltpu.VMEM((OWN, TILE, HDT), BF)
    dma = pltpu.SemaphoreType.DMA
    act = jax.ShapeDtypeStruct((OWN, TILE, HDT), BF)
    out, dq, dk, dv = pl.pallas_call(
        block_kernel,
        out_shape=[jax.ShapeDtypeStruct((ROWS, D), BF), act, act, act],
        in_specs=[S] * 4 + [V] * 2 + [A] * 6,
        out_specs=[A] * 4,
        scratch_shapes=[head, head, head, head, mid, pltpu.VMEM((HDT, D), BF), tok, tok, mid,
                        head, head, head, head,
                        pltpu.VMEM((TILES * SLOTS + 1, TILE, TILE), BF), pltpu.VMEM((SLOTS, TILE, TILE), F32),
                        pltpu.VMEM((TILES, TILE, TILE), BF), pltpu.VMEM((TILES, TILE, TILE), BF),
                        pltpu.VMEM((TILES, 1, TILE), F32), pltpu.VMEM((TXT + 1, TILE, TILE), F32),
                        dma((8, PEERS)), dma((8, PEERS)), dma((8,)), dma((8,)), dma((8,)), dma((2,))],
        compiler_params=pltpu.CompilerParams(collective_id=0, has_side_effects=True, vmem_limit_bytes=60 << 20),
        name="attention_block",
    )(*tabs, mod_gate, out_bias[None, :],
      *[x.reshape(OWN, TILE, HDT) for x in (queries, key_states, value_states)], residual[0], upstream[0], w_out)
    return (out[None], *[x.reshape(1, ROWS, HDT) for x in (dq, dk, dv)])


def solution(mesh):
    act = P("fsdp", "seq", None)
    return jax.shard_map(local, mesh=mesh, in_specs=(act,) * 5 + (P("fsdp", None), P(), P("fsdp", None), P(), P(), P()),
                         out_specs=(act,) * 4, check_vma=False)
```

time: 298 us -> 187 us (0.63)
  the two profiles are of different devices: /device:TPU:30 before, /device:TPU:85 now
where the time goes in v2:
time: 187 us; the launch traced here: 186 us
  Pallas kernels  175 us (94%)
  local copies, waits for them, and re-layouts  11.2 us (6%)
    pallas_call x1, Pallas kernels, local(): pl.pallas_call(block_kernel, out_shape=[jax.ShapeDtypeStruct((ROWS, D), B...  173 us
    unnamed x11, local copies, waits for them, and re-layouts  9.82 us

profile of v2, /device:TPU:85, one launch (start us, length us, event | category | flops | bytes accessed | tf_op | source)
XLA Modules:
  0.0 186.4 jit_solution(18129259492590709073)
XLA Ops:
  0.6 1.3 copy.16.count_ref
  2.0 1.4 copy.15.near_ref
  3.4 1.7 tables.1
  5.0 172.9 %attention_block.1 = (bf16[384,3072]{1,0:T(8,128)(2,1)}, bf16[3,128,2048]{2,1,0:T(8,128)(2,1)}, bf16[3,128,2048]{2,1,0:T(8,128)(2,1)}, bf16[3,128,2048]{2,1,0:T(8,128)(2,1)}) custom-call(s32[48,13]{1,0:T(8,128)} %get-tuple-element.12.keys_ref, f32[48,9]{1,0:T(8,128)} %get-tuple-element.13.bias_ref, s32[13,48]{1,0:T(8,128)} %get-tuple-element.14.pidx_ref, ...), custom_call_target="tpu_custom_call" | custom-call | tf_op jit(solution)/shard_map/attention_block/pallas_call | solution.py:328
  177.9 0.0 copy-start.2
  177.9 3.3 %copy.21 = bf16[1,384,3072]{2,1,0:T(8,128)(2,1)} copy(bf16[1,384,3072]{2,1,0:T(8,128)(2,1)} %bitcast.13) | data formatting | bytes 4718592
  181.3 0.0 copy-done.2
  181.3 0.0 copy-start.1
  181.3 1.1 copy.22
  182.4 0.8 copy-done.1
  183.3 0.0 copy-start
  183.3 1.1 copy.23
  184.4 0.8 copy-done
  185.2 1.1 copy.24
Async XLA Ops:
  177.9 3.4 %copy-start.2 = (bf16[3,128,2048]{2,1,0:T(8,128)(2,1)S(1)}, bf16[3,128,2048]{2,1,0:T(8,128)(2,1)}, u32[]{:S(2)}) copy-start(bf16[3,128,2048]{2,1,0:T(8,128)(2,1)} %get-tuple-element.17) | copy-start | bytes 4718596
  181.3 2.0 %copy-start.1 = (bf16[3,128,2048]{2,1,0:T(8,128)(2,1)S(1)}, bf16[3,128,2048]{2,1,0:T(8,128)(2,1)}, u32[]{:S(2)}) copy-start(bf16[3,128,2048]{2,1,0:T(8,128)(2,1)} %get-tuple-element.18) | copy-start | bytes 4718596
  183.3 2.0 %copy-start = (bf16[3,128,2048]{2,1,0:T(8,128)(2,1)S(1)}, bf16[3,128,2048]{2,1,0:T(8,128)(2,1)}, u32[]{:S(2)}) copy-start(bf16[3,128,2048]{2,1,0:T(8,128)(2,1)} %get-tuple-element.19) | copy-start | bytes 4718596

commit v3 on v2

--- a/solution.py
+++ b/solution.py
@@ -10,11 +10,13 @@
 EXP2 = FACTOR*math.log2(math.e)
 F32=jnp.float32; BF=jnp.bfloat16
 
-def table_kernel(text_ref, near_ref, near_t_ref, count_ref, count_t_ref, keys_ref, bias_ref, pidx_ref, tsel_ref):
-    near, near_t, count, count_t = near_ref[...], near_t_ref[...], count_ref[...], count_t_ref[...]
-    live = lax.broadcasted_iota(jnp.int32, (TILES, NBR), 1) < count
-    keys_ref[:, :NBR] = jnp.where(live, near, near[:, :1])
-    bias_ref[...] = jnp.where(live, 0.0, -jnp.inf).astype(F32)
+def fill_tables(text, near_ref, count_ref, pad_ref, keys_ref, bias_ref, pidx_ref, tsel_ref):
+    pad_ref[...] = jnp.zeros((TILE, TILE), jnp.int32)
+    pad_ref[:TILES, :NBR] = near_ref[...]
+    near, near_t = pad_ref[:TILES, :NBR], pad_ref[...].T[:NBR, :TILES]
+    count_t = count_ref[...]
+    pad_ref[:1, :TILES] = count_t
+    count = pad_ref[...].T[:TILES, :1]
     query = lax.broadcasted_iota(jnp.int32, (TILES, TILES), 0)
     key = lax.broadcasted_iota(jnp.int32, (TILES, TILES), 1)
     block = jnp.zeros((TILES, TILES), jnp.int32)
@@ -23,27 +25,22 @@
     ids = lax.broadcasted_iota(jnp.int32, (1, TILES), 1)
     tsel = jnp.full((1, TILES), TXT, jnp.int32)
     for u in range(TXT):
-        keys_ref[:, NBR + u:NBR + u + 1] = jnp.full((TILES, 1), text_ref[u], jnp.int32)
-        tsel = jnp.where(ids == text_ref[u], u, tsel)
-    tsel_ref[...] = tsel
+        tsel = jnp.where(ids == text[u], u, tsel)
+    tsel_ref[:1, :TILES] = tsel
     for r in range(SLOTS):
-        who = near_t[r:r + 1, :] if r < NBR else jnp.full((1, TILES), text_ref[r - NBR], jnp.int32)
+        live = r < count_t
+        if r < NBR:
+            who = near_t[r:r + 1, :]
+            keys_ref[r:r + 1, :TILES] = jnp.where(live, who, near_t[:1, :])
+            bias_ref[r:r + 1, :TILES] = jnp.where(live, 0.0, -jnp.inf).astype(F32)
+        else:
+            who = jnp.full((1, TILES), text[r - NBR], jnp.int32)
+            keys_ref[r:r + 1, :TILES] = who
         pick = jnp.sum(jnp.where(query == who, block, 0), axis=0, keepdims=True)
         ok = (pick > 0) & (tsel == TXT)
         if r < NBR:
-            ok = ok & (r < count_t)
-        pidx_ref[r:r + 1, :] = jnp.where(ok, pick - 1, TILES * SLOTS)
-
-
-def tables(neighbours, counts, text_tiles):
-    S, V = [pl.BlockSpec(memory_space=m) for m in (pltpu.SMEM, pltpu.VMEM)]
-    i32 = jnp.int32
-    return pl.pallas_call(
-        table_kernel,
-        out_shape=[jax.ShapeDtypeStruct((TILES, SLOTS), i32), jax.ShapeDtypeStruct((TILES, NBR), F32),
-                   jax.ShapeDtypeStruct((SLOTS, TILES), i32), jax.ShapeDtypeStruct((1, TILES), i32)],
-        in_specs=[S] + [V] * 4, out_specs=[V] * 4, name="tables",
-    )(text_tiles, neighbours, neighbours.T, counts[:, None], counts[None, :])
+            ok = ok & live
+        pidx_ref[r:r + 1, :TILES] = jnp.where(ok, pick - 1, TILES * SLOTS)
 
 
 def tile(ref, i):
@@ -58,7 +55,7 @@
 def fwd_tile(i, q_ref, k_ref, vt_ref, keys_ref, bias_ref, p_ref, s_ref, inv_ref, attn_ref):
     q = tile(q_ref, i)
     top = None
-    kc = jnp.concatenate([tile(k_ref, keys_ref[i, s]) for s in range(SLOTS)], axis=0)
+    kc = jnp.concatenate([tile(k_ref, keys_ref[s, i]) for s in range(SLOTS)], axis=0)
     sall = dot(kc, q, NT).reshape(SLOTS, TILE, TILE)
     for s in range(SLOTS):
         sc = sall[s]
@@ -68,7 +65,7 @@
     total = None
     parts = []
     for s in range(SLOTS):
-        shift = m if s < 3 or s >= NBR else m - bias_ref[i, s]
+        shift = m if s < 3 or s >= NBR else m - bias_ref[s, i]
         e = jnp.exp2(s_ref[s] * EXP2 - shift)
         total = e if total is None else total + e
         e16 = e.astype(BF)
@@ -77,13 +74,13 @@
     inv = 1.0 / jnp.sum(total, axis=0, keepdims=True)
     inv_ref[i] = inv
     pt = jnp.concatenate(parts, axis=0)
-    vt = jnp.concatenate([vt_ref[keys_ref[i, s]] for s in range(SLOTS)], axis=1)
+    vt = jnp.concatenate([vt_ref[keys_ref[s, i]] for s in range(SLOTS)], axis=1)
     attn_t = dot(vt, pt) * inv
     attn_ref[i] = attn_t.astype(BF).T
 
 def key_tile(j, who_ref, pidx_ref, tsel_ref, p_ref, x_ref, text_ref, out_ref):
     lhs = jnp.concatenate([p_ref[pidx_ref[r, j]] for r in range(SLOTS)], axis=1)
-    rhs = jnp.concatenate([tile(x_ref, who_ref[j, r]) for r in range(SLOTS)], axis=0)
+    rhs = jnp.concatenate([tile(x_ref, who_ref[r, j]) for r in range(SLOTS)], axis=0)
     acc = dot(lhs, rhs) + text_ref[tsel_ref[0, j]]
     out_ref[j] = acc.astype(BF)
 
@@ -104,12 +101,12 @@
     delta = jnp.sum(prod.T, axis=0, keepdims=True)
     c = inv_ref[i] * FACTOR
     dc = delta * c
-    vc = jnp.concatenate([tile(v_ref, keys_ref[i, s]) for s in range(SLOTS)], axis=0)
+    vc = jnp.concatenate([tile(v_ref, keys_ref[s, i]) for s in range(SLOTS)], axis=0)
     dpall = dot(vc, do, NT).reshape(SLOTS, TILE, TILE)
     parts = [(p_ref[i * SLOTS + s].astype(F32) * (dpall[s] * c - dc)).astype(BF) for s in range(SLOTS)]
     for s in range(SLOTS): p_ref[i * SLOTS + s] = parts[s]
     ds = jnp.concatenate(parts, axis=0)
-    kt = jnp.concatenate([kt_ref[keys_ref[i, s]] for s in range(SLOTS)], axis=1)
+    kt = jnp.concatenate([kt_ref[keys_ref[s, i]] for s in range(SLOTS)], axis=1)
     dq_t = dot(kt, ds)
     dq_ref[i] = dq_t.astype(BF).T
 
@@ -134,12 +131,13 @@
     return pl.ds(pl.multiple_of(p * HD, HD), HD)
 
 
-def block_kernel(keys_ref, bias_ref, pidx_ref, tsel_ref, gate_ref, obias_ref,
+def block_kernel(text_tiles, near_ref, count_ref, gate_ref, obias_ref,
                  q_in, k_in, v_in, res_in, up_in, w_in,
-                 out_ref, dq_out, dk_out, dv_out,
-                 q_ref, k_ref, v_ref, do_ref, at_land, w_ref, up_ref, sc_ref, dst_ref,
-                 at_st, dv_st, dq_st, dk_st,
+                 sc_ref, dq_out, dk_out, dv_out,
+                 q_ref, k_ref, v_ref, do_ref, at_land, w_ref, up_ref, dst_ref,
+                 at_st, dq_st,
                  p_ref, s_ref, kt_ref, vt_ref, inv_ref, text_ref,
+                 keys_ref, bias_ref, pidx_ref, tsel_ref, keys_v, bias_v, pidx_v, tsel_v, pad_ref,
                  send, recv, own, wsend, wrecv, lsem):
     me = lax.axis_index("seq")
     mx, mz = me // 4, me % 4
@@ -151,6 +149,7 @@
     far = ((y + 2) % 4) * 2 + c
 
     def peer(n):
+        n = (n * 7) % PEERS
         return ((mx + n // 4) % 4) * 4 + (mz + n % 4) % 4
 
     def loop(n, body, lo=0):
@@ -185,6 +184,8 @@
         part = w_ref.at[wrows(shard, off, n)]
         return pltpu.make_async_remote_copy(part if src is None else src, part, wsend.at[k], wrecv.at[k],
                                             device_id={"fsdp": target}, device_id_type=MESH)
+
+    dv_st, dk_st = k_ref, do_ref
 
     get_up = pltpu.make_async_copy(up_in, up_ref, lsem.at[0])
     get_up.start()
@@ -207,6 +208,11 @@
         own_head(a, src, land).start()
         loop(PEERS, lambda n, a=a, src=src, land=land: to_head(a, src, land, peer(n)).start(), 1)
 
+    fill_tables([text_tiles[u] for u in range(TXT)], near_ref, count_ref, pad_ref, keys_v, bias_v, pidx_v, tsel_v)
+    moves = [pltpu.make_async_copy(a, b, lsem.at[2 + k]) for k, (a, b) in enumerate(
+        ((keys_v, keys_ref), (bias_v, bias_ref), (pidx_v, pidx_ref), (tsel_v, tsel_ref)))]
+    for move in moves:
+        move.start()
     p_ref[TILES * SLOTS] = jnp.zeros((TILE, TILE), BF)
     get_up.wait()
 
@@ -222,6 +228,8 @@
         r = dot(sc_ref[...], w_ref[wrows(shard), :], NT).astype(BF)
         dst_ref[:, :, pl.ds(pl.multiple_of(shard * SHARD, SHARD), SHARD)] = r.reshape(OWN, TILE, SHARD)
 
+    for move in moves:
+        move.wait()
     get_w.wait()
     d_attn(f)
     w_sib.wait_recv()
@@ -256,32 +264,38 @@
     d_attn(ydn + 1 - 2 * c)
     sh_up.wait_recv()
     d_attn(yup + 1 - 2 * c)
+    own_head(Q_, q_in, q_ref).wait()
+    loop(PEERS, lambda n: got_head(Q_, q_in, q_ref, peer(n)), 1)
+
+    def stage(a, st, land, per_tile, lo=1, hi=PEERS + 1):
+        def body(n):
+            p = peer(n)
+            for t in range(3):
+                per_tile(p * 3 + t)
+
+            @pl.when(n < PEERS)
+            def _():
+                to_rows(a, st, land, p).start()
+
+        loop(hi, body, lo)
+        if hi > PEERS:
+            own_rows(a, st, land).start()
+
+    def forward(lo, hi):
+        stage(AT_, at_st, at_land, lambda i: fwd_tile(i, q_ref, k_ref, vt_ref, keys_ref, bias_ref, p_ref, s_ref, inv_ref, at_st), lo, hi)
+
+    forward(1, 4)
     wcopy(2, far, yup, None, 0, 128).wait_recv()
     wcopy(3, far, yup, None, 128, 128).wait_recv()
     sh_far = wcopy(7, far, sib)
     sh_far.start()
+    forward(4, 7)
     d_attn(far)
-    own_head(Q_, q_in, q_ref).wait()
-    loop(PEERS, lambda n: got_head(Q_, q_in, q_ref, peer(n)), 1)
     sh_far.wait_recv()
     d_attn(far + 1 - 2 * c)
+    loop(PEERS, lambda n: to_head(O_, dst_ref, do_ref, peer(n)).start(), 1)
     own_head(O_, dst_ref, do_ref).start()
-    loop(PEERS, lambda n: to_head(O_, dst_ref, do_ref, peer(n)).start(), 1)
-
-    def stage(a, st, land, per_tile):
-        def body(n):
-            p = peer(n)
-            for t in range(3):
-                per_tile(p * 3 + t)
-
-            @pl.when(n < PEERS)
-            def _():
-                to_rows(a, st, land, p).start()
-
-        loop(PEERS + 1, body, 1)
-        own_rows(a, st, land).start()
-
-    stage(AT_, at_st, at_land, lambda i: fwd_tile(i, q_ref, k_ref, vt_ref, keys_ref, bias_ref, p_ref, s_ref, inv_ref, at_st))
+    forward(7, PEERS + 1)
     own_head(O_, dst_ref, do_ref).wait()
     loop(PEERS, lambda n: got_head(O_, dst_ref, do_ref, peer(n)), 1)
     lax.fori_loop(0, TILES, lambda i, _: (scale_rows(i, do_ref, inv_ref, dq_st), 0)[1], 0, unroll=4)
@@ -301,8 +315,6 @@
         sc_ref[:, sl] = (up_ref[:, sl].astype(F32) + gate_ref[:, sl] * acc).astype(BF)
 
     loop(D // 256, project)
-    put = pltpu.make_async_copy(sc_ref, out_ref, lsem.at[1])
-    put.start()
 
     outs = ((DV_, dv_st, dv_out), (DQ_, dq_st, dq_out), (DK_, dk_st, dk_out))
     for a, st, land in outs:
@@ -314,31 +326,32 @@
         loop(PEERS, lambda n, a=a, src=src, land=land: to_head(a, src, land, peer(n)).wait_send(), 1)
     for a, st, land in ((AT_, at_st, at_land),) + outs:
         loop(PEERS, lambda n, a=a, st=st, land=land: to_rows(a, st, land, peer(n)).wait_send(), 1)
-    put.wait()
 
 
 def local(queries, key_states, value_states, residual, upstream, mod_gate, out_bias, w_out, neighbours, counts, text_tiles):
-    tabs = tables(neighbours, counts, text_tiles)
     S, V, A = [pl.BlockSpec(memory_space=m) for m in (pltpu.SMEM, pltpu.VMEM, pl.ANY)]
     head = pltpu.VMEM((TILES, TILE, HD), BF)
     tok = pltpu.VMEM((ROWS, D), BF)
     mid = pltpu.VMEM((OWN, TILE, HDT), BF)
     dma = pltpu.SemaphoreType.DMA
+    i32 = jnp.int32
     act = jax.ShapeDtypeStruct((OWN, TILE, HDT), BF)
     out, dq, dk, dv = pl.pallas_call(
         block_kernel,
-        out_shape=[jax.ShapeDtypeStruct((ROWS, D), BF), act, act, act],
-        in_specs=[S] * 4 + [V] * 2 + [A] * 6,
-        out_specs=[A] * 4,
-        scratch_shapes=[head, head, head, head, mid, pltpu.VMEM((HDT, D), BF), tok, tok, mid,
-                        head, head, head, head,
+        out_shape=[tok, mid, mid, mid],
+        in_specs=[S] + [V] * 4 + [A] * 6,
+        out_specs=[V] * 4,
+        scratch_shapes=[head, head, head, head, mid, pltpu.VMEM((HDT, D), BF), tok, mid,
+                        head, head,
                         pltpu.VMEM((TILES * SLOTS + 1, TILE, TILE), BF), pltpu.VMEM((SLOTS, TILE, TILE), F32),
                         pltpu.VMEM((TILES, TILE, TILE), BF), pltpu.VMEM((TILES, TILE, TILE), BF),
                         pltpu.VMEM((TILES, 1, TILE), F32), pltpu.VMEM((TXT + 1, TILE, TILE), F32),
-                        dma((8, PEERS)), dma((8, PEERS)), dma((8,)), dma((8,)), dma((8,)), dma((2,))],
-        compiler_params=pltpu.CompilerParams(collective_id=0, has_side_effects=True, vmem_limit_bytes=60 << 20),
+                        *[m((n, TILE), t) for m in (pltpu.SMEM, pltpu.VMEM) for n, t in ((16, i32), (16, F32), (16, i32), (8, i32))],
+                        pltpu.VMEM((TILE, TILE), i32),
+                        dma((8, PEERS)), dma((8, PEERS)), dma((8,)), dma((8,)), dma((8,)), dma((6,))],
+        compiler_params=pltpu.CompilerParams(collective_id=0, has_side_effects=True, vmem_limit_bytes=54 << 20),
         name="attention_block",
-    )(*tabs, mod_gate, out_bias[None, :],
+    )(text_tiles, neighbours, counts[None, :], mod_gate, out_bias[None, :],
       *[x.reshape(OWN, TILE, HDT) for x in (queries, key_states, value_states)], residual[0], upstream[0], w_out)
     return (out[None], *[x.reshape(1, ROWS, HDT) for x in (dq, dk, dv)])
 

time: 187 us -> 177 us (0.947)
  the two profiles are of different devices: /device:TPU:85 before, /device:TPU:30 now
where the time goes in v3:
time: 177 us; the launch traced here: 176 us
  Pallas kernels  169 us (95%)
  local copies, waits for them, and re-layouts  6.22 us (4%)
    pallas_call x1, Pallas kernels, local(): pl.pallas_call(block_kernel, out_shape=[tok, mid, mid, mid], in_specs=[S]...  169 us
    unnamed x5, local copies, waits for them, and re-layouts  6.22 us

profile of v3, /device:TPU:30, one launch (start us, length us, event | category | flops | bytes accessed | tf_op | source)
XLA Modules:
  0.0 176.3 jit_solution(6777362869795204617)
XLA Ops:
  0.6 1.4 copy.15.near_ref
  2.0 169.5 %attention_block.1 = (bf16[384,3072]{1,0:T(8,128)(2,1)S(1)}, bf16[3,128,2048]{2,1,0:T(8,128)(2,1)S(1)}, bf16[3,128,2048]{2,1,0:T(8,128)(2,1)S(1)}, bf16[3,128,2048]{2,1,0:T(8,128)(2,1)S(1)}) custom-call(s32[4]{0:T(128)} %text_tiles.1, s32[48,9]{1,0:T(8,128)} %copy.15.near_ref, s32[1,48]{1,0:T(1,128)} %bitcast.21, f32[1,3072]{1,0:T(1,128)} %gate_ref.1, ...), custom_call_target="tpu_custom_call" | custom-call | tf_op jit(solution)/shard_map/attention_block/pallas_call | solution.py:339
  171.5 1.4 copy.20
  172.9 1.1 copy.21
  174.0 1.1 copy.22
  175.2 1.1 copy.23

commit v4 on v3

--- a/solution.py
+++ b/solution.py
@@ -12,8 +12,9 @@
 
 def fill_tables(text, near_ref, count_ref, pad_ref, keys_ref, bias_ref, pidx_ref, tsel_ref):
     pad_ref[...] = jnp.zeros((TILE, TILE), jnp.int32)
-    pad_ref[:TILES, :NBR] = near_ref[...]
-    near, near_t = pad_ref[:TILES, :NBR], pad_ref[...].T[:NBR, :TILES]
+    near_t = near_ref[...]
+    pad_ref[:NBR, :TILES] = near_t
+    near = pad_ref[...].T[:TILES, :NBR]
     count_t = count_ref[...]
     pad_ref[:1, :TILES] = count_t
     count = pad_ref[...].T[:TILES, :1]
@@ -149,7 +150,7 @@
     far = ((y + 2) % 4) * 2 + c
 
     def peer(n):
-        n = (n * 7) % PEERS
+        n = (n * 11) % PEERS
         return ((mx + n // 4) % 4) * 4 + (mz + n % 4) % 4
 
     def loop(n, body, lo=0):
@@ -282,14 +283,27 @@
             own_rows(a, st, land).start()
 
     def forward(lo, hi):
-        stage(AT_, at_st, at_land, lambda i: fwd_tile(i, q_ref, k_ref, vt_ref, keys_ref, bias_ref, p_ref, s_ref, inv_ref, at_st), lo, hi)
-
-    forward(1, 4)
+        def pair(k):
+            a, b = peer(lo + 2 * k), peer(lo + 2 * k + 1)
+            for p in (a, b):
+                for t in range(3):
+                    fwd_tile(p * 3 + t, q_ref, k_ref, vt_ref, keys_ref, bias_ref, p_ref, s_ref, inv_ref, at_st)
+            to_rows(AT_, at_st, at_land, a).start()
+
+            @pl.when(lo + 2 * k + 1 < PEERS)
+            def _():
+                to_rows(AT_, at_st, at_land, b).start()
+
+        loop((hi - lo) // 2, pair)
+        if hi > PEERS:
+            own_rows(AT_, at_st, at_land).start()
+
+    forward(1, 3)
     wcopy(2, far, yup, None, 0, 128).wait_recv()
     wcopy(3, far, yup, None, 128, 128).wait_recv()
     sh_far = wcopy(7, far, sib)
     sh_far.start()
-    forward(4, 7)
+    forward(3, 7)
     d_attn(far)
     sh_far.wait_recv()
     d_attn(far + 1 - 2 * c)
@@ -351,7 +365,7 @@
                         dma((8, PEERS)), dma((8, PEERS)), dma((8,)), dma((8,)), dma((8,)), dma((6,))],
         compiler_params=pltpu.CompilerParams(collective_id=0, has_side_effects=True, vmem_limit_bytes=54 << 20),
         name="attention_block",
-    )(text_tiles, neighbours, counts[None, :], mod_gate, out_bias[None, :],
+    )(text_tiles, neighbours.T, counts[None, :], mod_gate, out_bias[None, :],
       *[x.reshape(OWN, TILE, HDT) for x in (queries, key_states, value_states)], residual[0], upstream[0], w_out)
     return (out[None], *[x.reshape(1, ROWS, HDT) for x in (dq, dk, dv)])
 

time: 177 us -> 168 us (0.949)
  Pallas kernels: 169 us -> 161 us
    pallas_call x1, Pallas kernels: 169 us -> 161 us  [local(): pl.pallas_call(block_kernel, out_shape=[tok, mid, mid, mid], in_specs=[S]...]
    unnamed x5 -> x4, local copies, waits for them, and re-layouts: 6.22 us -> 4.83 us
where the time goes in v4:
time: 168 us; the launch traced here: 166 us
  Pallas kernels  161 us (96%)
  local copies, waits for them, and re-layouts  4.83 us (3%)
    pallas_call x1, Pallas kernels, local(): pl.pallas_call(block_kernel, out_shape=[tok, mid, mid, mid], in_specs=[S]...  161 us
    unnamed x4, local copies, waits for them, and re-layouts  4.83 us

profile of v4, /device:TPU:30, one launch (start us, length us, event | category | flops | bytes accessed | tf_op | source)
XLA Modules:
  0.0 166.2 jit_solution(14131827964279143269)
XLA Ops:
  0.6 160.7 %attention_block.1 = (bf16[384,3072]{1,0:T(8,128)(2,1)S(1)}, bf16[3,128,2048]{2,1,0:T(8,128)(2,1)S(1)}, bf16[3,128,2048]{2,1,0:T(8,128)(2,1)S(1)}, bf16[3,128,2048]{2,1,0:T(8,128)(2,1)S(1)}) custom-call(s32[4]{0:T(128)} %text_tiles.1, s32[9,48]{1,0:T(8,128)} %bitcast.22, s32[1,48]{1,0:T(1,128)} %bitcast.23, f32[1,3072]{1,0:T(1,128)} %gate_ref.1, ...), custom_call_target="tpu_custom_call" | custom-call | tf_op jit(solution)/shard_map/attention_block/pallas_call | solution.py:353
  161.3 1.4 copy.19
  162.7 1.1 copy.20
  163.9 1.1 copy.21
  165.0 1.1 copy.22

commit v5 on v4

--- a/solution.py
+++ b/solution.py
@@ -269,34 +269,23 @@
     loop(PEERS, lambda n: got_head(Q_, q_in, q_ref, peer(n)), 1)
 
     def stage(a, st, land, per_tile, lo=1, hi=PEERS + 1):
-        def body(n):
-            p = peer(n)
-            for t in range(3):
-                per_tile(p * 3 + t)
-
-            @pl.when(n < PEERS)
+        def pair(k):
+            a_p, b_p = peer(lo + 2 * k), peer(lo + 2 * k + 1)
+            for p in (a_p, b_p):
+                for t in range(3):
+                    per_tile(p * 3 + t)
+            to_rows(a, st, land, a_p).start()
+
+            @pl.when(lo + 2 * k + 1 < PEERS)
             def _():
-                to_rows(a, st, land, p).start()
-
-        loop(hi, body, lo)
+                to_rows(a, st, land, b_p).start()
+
+        loop((hi - lo) // 2, pair)
         if hi > PEERS:
             own_rows(a, st, land).start()
 
     def forward(lo, hi):
-        def pair(k):
-            a, b = peer(lo + 2 * k), peer(lo + 2 * k + 1)
-            for p in (a, b):
-                for t in range(3):
-                    fwd_tile(p * 3 + t, q_ref, k_ref, vt_ref, keys_ref, bias_ref, p_ref, s_ref, inv_ref, at_st)
-            to_rows(AT_, at_st, at_land, a).start()
-
-            @pl.when(lo + 2 * k + 1 < PEERS)
-            def _():
-                to_rows(AT_, at_st, at_land, b).start()
-
-        loop((hi - lo) // 2, pair)
-        if hi > PEERS:
-            own_rows(AT_, at_st, at_land).start()
+        stage(AT_, at_st, at_land, lambda i: fwd_tile(i, q_ref, k_ref, vt_ref, keys_ref, bias_ref, p_ref, s_ref, inv_ref, at_st), lo, hi)
 
     forward(1, 3)
     wcopy(2, far, yup, None, 0, 128).wait_recv()

time: 168 us -> 168 us (level)
  no operation moved by 1% of the time
where the time goes in v5:
time: 168 us; the launch traced here: 167 us
  Pallas kernels  162 us (96%)
  local copies, waits for them, and re-layouts  4.83 us (3%)
    pallas_call x1, Pallas kernels, local(): pl.pallas_call(block_kernel, out_shape=[tok, mid, mid, mid], in_specs=[S]...  162 us
    unnamed x4, local copies, waits for them, and re-layouts  4.83 us

profile of v5, /device:TPU:30, one launch (start us, length us, event | category | flops | bytes accessed | tf_op | source)
XLA Modules:
  0.0 167.4 jit_solution(649702223724736151)
XLA Ops:
  0.6 162.0 %attention_block.1 = (bf16[384,3072]{1,0:T(8,128)(2,1)S(1)}, bf16[3,128,2048]{2,1,0:T(8,128)(2,1)S(1)}, bf16[3,128,2048]{2,1,0:T(8,128)(2,1)S(1)}, bf16[3,128,2048]{2,1,0:T(8,128)(2,1)S(1)}) custom-call(s32[4]{0:T(128)} %text_tiles.1, s32[9,48]{1,0:T(8,128)} %bitcast.22, s32[1,48]{1,0:T(1,128)} %bitcast.23, f32[1,3072]{1,0:T(1,128)} %gate_ref.1, ...), custom_call_target="tpu_custom_call" | custom-call | tf_op jit(solution)/shard_map/attention_block/pallas_call | solution.py:342
  162.6 1.4 copy.19
  164.0 1.1 copy.20
  165.2 1.1 copy.21
  166.3 1.1 copy.22
